TPU v7x, 32 devices: a whole 2x2x4 slice. The times are simulated.
32 devices in a mesh: shot: 8 (over z, x), line: 4 (over y, core).
Axes of the slice: x: 2, y: 2, z: 4, core: 2. Of those that a mesh axis runs over, the one named last changes fastest.
Arguments:
- traces: bfloat16 [16384, 2048], P(('shot', 'line')), may hold values from -12 to 12
- targets: bfloat16 [16384, 2048], P(('shot', 'line')), may hold values from -64 to 64
- src_local: int32 [16384], P(('shot', 'line')), may hold values from 0 to 3
- rcv_term: int32 [16384], P(('shot', 'line')), may hold values from 0 to 4095, as said below
- cmp_term: int32 [16384], P(('shot', 'line')), may hold values from 0 to 8191, as said below
- rcv_home: int32 [4096], replicated, may hold values from 0 to 4095, as said below
- cmp_home: int32 [8192], replicated, may hold values from 0 to 8191, as said below
- counts: int32 [32], P(('shot', 'line')), may hold values from 128 to 512, as said below
- src_filters: float32 [128, 128], P(('shot', 'line')), may hold values from -1.75 to 1.75
- rcv_filters: float32 [4096, 128], P(('shot', 'line')), may hold values from -1.75 to 1.75
- cmp_filters: float32 [8192, 128], P(('shot', 'line')), may hold values from -1.75 to 1.75
Outputs:
- src_out: float32 [128, 128], P(('shot', 'line'))
- rcv_out: float32 [4096, 128], P(('shot', 'line'))
- cmp_out: float32 [8192, 128], P(('shot', 'line'))
Inputs may be any that keep to these rules, and one draw needn't show every extreme that they name: Receiver row rcv_home[rcv_term[t]] lies on device rcv_home[rcv_term[t]] // 128. Among the 512 trace slots of one device (live or not) at most 32 have receiver rows on any one device; in every draw some device holds the receiver rows of exactly 32 slots of every device. `cmp_term`: likewise for CMP rows with 256 rows a device: at most 32 slots of one device name CMP rows on any one device, and some device is named so by exactly 32 slots of every device. `rcv_home`: A permutation of 0 to 4095. `cmp_home`: A permutation of 0 to 8191. The first counts[d] slots of device d are live; some device is full.
All inputs are finite; a program needn't handle non-finite values.
Results may differ from a plain program's by a relative error of at most 0.0027.
Values sent between devices are 32-bit elements; how exact they have to be, the bound alone decides.
A program may use at most 64 MiB of HBM per device.

v0:
```python
import jax
import jax.numpy as jnp
from jax import lax
from jax.sharding import PartitionSpec as P

TBLK = 32


step_size = 0.5
highest = lax.Precision.HIGHEST


def pick_rows(table_rows, slot_index):
    flat_index = slot_index.reshape(-1)
    onehot = (
        flat_index[:, None] == jnp.arange(table_rows.shape[0], dtype=jnp.int32)[None, :]
    ).astype(jnp.float32)
    picked = jnp.dot(onehot, table_rows, precision=highest, preferred_element_type=jnp.float32)
    return picked.reshape(slot_index.shape + (table_rows.shape[1],))


def add_rows(slot_index, values, term_count):
    onehot = (
        slot_index.reshape(-1)[None, :] == jnp.arange(term_count, dtype=jnp.int32)[:, None]
    ).astype(jnp.float32)
    return jnp.dot(
        onehot,
        values.reshape(onehot.shape[1], -1),
        precision=highest,
        preferred_element_type=jnp.float32,
    )


def send_slots(slot_rows, terms_dev, device_count, slot_cap):
    owner_dev = slot_rows // terms_dev
    place_row = slot_rows % terms_dev
    onehot = (owner_dev[:, None] == jnp.arange(device_count, dtype=jnp.int32)[None, :]).astype(
        jnp.int32
    )
    before = jnp.cumsum(onehot, axis=0) - onehot
    rank_rows = jnp.sum(before * onehot, axis=1)
    slot_index = owner_dev * slot_cap + rank_rows
    request = jnp.zeros((device_count * slot_cap,), jnp.int32).at[slot_index].set(place_row)
    return (slot_index, request.reshape(device_count, slot_cap))


def settle(filter_table, slot_index, grad_in, power_in):
    term_count = filter_table.shape[0]
    sum_rows = add_rows(slot_index, grad_in, term_count)
    energy = add_rows(slot_index, power_in, term_count)[:, 0]
    return filter_table - step_size * sum_rows / jnp.maximum(energy, 1.0)[:, None]


def diagonal_sums(cross_before, cross_now):
    row_count, tap_count = (cross_now.shape[0], cross_now.shape[1])
    joined = jnp.concatenate([cross_before, cross_now], axis=2).reshape(
        row_count, 2 * tap_count * tap_count
    )
    padded = jnp.concatenate([joined, jnp.zeros((row_count, tap_count), jnp.float32)], axis=1)
    skewed = padded.reshape(row_count, tap_count, 2 * tap_count + 1)
    column_sums = jnp.sum(skewed, axis=1)
    return column_sums[:, 1 : tap_count + 1][:, ::-1]


def body(
    traces,
    targets,
    src_local,
    rcv_term,
    cmp_term,
    rcv_home,
    cmp_home,
    counts,
    src_filters,
    rcv_filters,
    cmp_filters,
):
    trace_rows, samples = traces.shape
    tap_count = src_filters.shape[1]
    device_count = lax.axis_size(("shot", "line"))
    slot_cap = max(2, 2 * trace_rows // device_count)
    rcv_index, rcv_request = send_slots(
        rcv_home[rcv_term], rcv_filters.shape[0], device_count, slot_cap
    )
    cmp_index, cmp_request = send_slots(
        cmp_home[cmp_term], cmp_filters.shape[0], device_count, slot_cap
    )
    requests = jnp.stack([rcv_request, cmp_request])
    received = lax.all_to_all(requests, ("shot", "line"), split_axis=1, concat_axis=1, tiled=True)
    values = jnp.stack([pick_rows(rcv_filters, received[0]), pick_rows(cmp_filters, received[1])])
    fetched = lax.all_to_all(values, ("shot", "line"), split_axis=1, concat_axis=1, tiled=True)
    fetched_rows = fetched.reshape(2, device_count * slot_cap, tap_count)
    src_onehot = (
        src_local[:, None] == jnp.arange(src_filters.shape[0], dtype=jnp.int32)[None, :]
    ).astype(jnp.float32)
    src_part = jnp.dot(
        src_onehot, src_filters, precision=highest, preferred_element_type=jnp.float32
    )
    mixed_filters = (src_part + fetched_rows[0][rcv_index] + fetched_rows[1][cmp_index]).astype(
        jnp.bfloat16
    )
    live_mask = (jnp.arange(trace_rows, dtype=jnp.int32) < counts[0]).astype(jnp.float32)
    block_count = samples // tap_count
    tap_range = jnp.arange(tap_count, dtype=jnp.int32)
    lag_index = tap_range[:, None, None]
    row_tap = tap_range[None, :, None]
    col_tap = tap_range[None, None, :]
    shift_upper = (col_tap - row_tap == lag_index).astype(jnp.bfloat16)
    shift_lower = (col_tap - row_tap + tap_count == lag_index).astype(jnp.bfloat16)

    def one_block(turn_index, carry):
        grad_rows, powers = carry
        start_row = turn_index * TBLK
        trace_block = lax.dynamic_slice_in_dim(traces, start_row, TBLK, 0).reshape(
            TBLK, block_count, tap_count
        )
        filter_block = lax.dynamic_slice_in_dim(mixed_filters, start_row, TBLK, 0)
        upper = jnp.einsum(
            "rk,kji->rji", filter_block, shift_upper, preferred_element_type=jnp.float32
        ).astype(jnp.bfloat16)
        lower = jnp.einsum(
            "rk,kji->rji", filter_block, shift_lower, preferred_element_type=jnp.float32
        ).astype(jnp.bfloat16)
        current = jnp.einsum("rbj,rji->rbi", trace_block, upper, preferred_element_type=jnp.float32)
        carried = jnp.einsum("rbj,rji->rbi", trace_block, lower, preferred_element_type=jnp.float32)
        model_block = current + jnp.concatenate(
            [jnp.zeros((TBLK, 1, tap_count), jnp.float32), carried[:, :-1]], axis=1
        )
        target_block = lax.dynamic_slice_in_dim(targets, start_row, TBLK, 0).reshape(
            TBLK, block_count, tap_count
        )
        alive_rows = lax.dynamic_slice_in_dim(live_mask, start_row, TBLK, 0)
        misfit = (
            alive_rows[:, None, None] * (model_block - target_block.astype(jnp.float32))
        ).astype(jnp.bfloat16)
        later = jnp.concatenate(
            [misfit[:, 1:], jnp.zeros((TBLK, 1, tap_count), jnp.bfloat16)], axis=1
        )
        cross_now = jnp.einsum(
            "rbi,rbj->rij", misfit, trace_block, preferred_element_type=jnp.float32
        )
        cross_before = jnp.einsum(
            "rbi,rbj->rij", later, trace_block, preferred_element_type=jnp.float32
        )
        grad_block = diagonal_sums(cross_before, cross_now)
        energy = alive_rows * jnp.sum(jnp.square(trace_block.astype(jnp.float32)), axis=(1, 2))
        grad_rows = lax.dynamic_update_slice_in_dim(grad_rows, grad_block, start_row, 0)
        powers = lax.dynamic_update_slice_in_dim(powers, energy, start_row, 0)
        return (grad_rows, powers)

    turn_count = trace_rows // TBLK
    grad_rows, powers = lax.fori_loop(
        0,
        turn_count,
        one_block,
        (jnp.zeros((trace_rows, tap_count), jnp.float32), jnp.zeros((trace_rows,), jnp.float32)),
    )
    empty_grad = jnp.zeros((device_count * slot_cap, tap_count), jnp.float32)
    empty_power = jnp.zeros((device_count * slot_cap,), jnp.float32)
    send_grad = jnp.stack(
        [empty_grad.at[rcv_index].set(grad_rows), empty_grad.at[cmp_index].set(grad_rows)]
    )
    send_power = jnp.stack(
        [empty_power.at[rcv_index].set(powers), empty_power.at[cmp_index].set(powers)]
    )
    got_grad, got_power = (
        lax.all_to_all(
            send_grad.reshape(2, device_count, slot_cap, tap_count),
            ("shot", "line"),
            split_axis=1,
            concat_axis=1,
            tiled=True,
        ),
        lax.all_to_all(
            send_power.reshape(2, device_count, slot_cap),
            ("shot", "line"),
            split_axis=1,
            concat_axis=1,
            tiled=True,
        ),
    )
    src_out = settle(src_filters, src_local, grad_rows, powers)
    rcv_out = settle(rcv_filters, received[0], got_grad[0], got_power[0])
    cmp_out = settle(cmp_filters, received[1], got_grad[1], got_power[1])
    return (src_out, rcv_out, cmp_out)


def solution(mesh):
    return jax.shard_map(
        body,
        mesh=mesh,
        in_specs=(
            P(("shot", "line"), None),
            P(("shot", "line"), None),
            P(("shot", "line")),
            P(("shot", "line")),
            P(("shot", "line")),
            P(),
            P(),
            P(("shot", "line")),
            P(("shot", "line"), None),
            P(("shot", "line"), None),
            P(("shot", "line"), None),
        ),
        out_specs=(P(("shot", "line"), None), P(("shot", "line"), None), P(("shot", "line"), None)),
        check_vma=False,
    )
```

profile of v0, /device:TPU:0, one launch (start us, length us, event | category | flops | bytes accessed | tf_op | source)
XLA Modules:
  0.0 589.7 jit_solution(4007084186912735095)
XLA Ops:
  17.0 14.4 %all_to_all.20 = s32[2,32,32]{2,0,1:T(2,128)S(1)} all-to-all(s32[2,32,32]{2,0,1:T(2,128)S(1)} %pad_add_fusion), channel_id=1, replica_groups=mesh['shot'=8,'line'=4] {'shot','line'}, dimensions={1} | all-to-all | bytes 16384 | tf_op jit(solution)/shard_map/all_to_all | solution.py:89
  37.5 25.3 %all-to-all-done.1 = f32[2,32,32,128]{3,2,0,1:T(8,128)S(1)} async-done(((f32[2,32,32,128]{3,2,0,1:T(8,128)}), f32[2,32,32,128]{3,2,0,1:T(8,128)S(1)}, u32[]{:S(2)}, u32[]{:S(2)}) %all-to-all-start.1) | async-done | bytes 1048608 | tf_op jit(solution)/shard_map/all_to_all | solution.py:91
  65.4 472.7 %while.16 = (s32[]{:T(128)}, f32[512,128]{1,0:T(8,128)S(1)}, f32[512]{0:T(512)S(1)}, f32[512]{0:T(512)S(1)}, bf16[512,2048]{1,0:T(8,128)(2,1)}, /*index=5*/bf16[...) while((s32[]{:T(128)}, f32[512,128]{1,0:T(8,128)S(1)}, ...), condition=%wide.region_11.12_spmd.clone, body=%wide.region_8.11_spmd.clone.sunk | while | flops 346550240 | bytes 49965648 | solution.py:152
  83.5 8.0 %reshape.421 = f32[32,128,257]{2,1,0:T(8,128)} reshape(f32[32,32896]{1,0:T(8,128)} %concatenate.36) | data formatting | bytes 8421376 | tf_op jit(solution)/shard_map/while/body/eval_jaxpr/reshape | solution.py:60
  113.0 8.0 %reshape.421 = f32[32,128,257]{2,1,0:T(8,128)} reshape(f32[32,32896]{1,0:T(8,128)} %concatenate.36) | data formatting | bytes 8421376 | tf_op jit(solution)/shard_map/while/body/eval_jaxpr/reshape | solution.py:60
  132.7 5.4 copy.45
  142.6 8.0 %reshape.421 = f32[32,128,257]{2,1,0:T(8,128)} reshape(f32[32,32896]{1,0:T(8,128)} %concatenate.36) | data formatting | bytes 8421376 | tf_op jit(solution)/shard_map/while/body/eval_jaxpr/reshape | solution.py:60
  172.1 8.0 %reshape.421 = f32[32,128,257]{2,1,0:T(8,128)} reshape(f32[32,32896]{1,0:T(8,128)} %concatenate.36) | data formatting | bytes 8421376 | tf_op jit(solution)/shard_map/while/body/eval_jaxpr/reshape | solution.py:60
  201.7 8.0 %reshape.421 = f32[32,128,257]{2,1,0:T(8,128)} reshape(f32[32,32896]{1,0:T(8,128)} %concatenate.36) | data formatting | bytes 8421376 | tf_op jit(solution)/shard_map/while/body/eval_jaxpr/reshape | solution.py:60
  221.3 5.4 copy.45
  231.2 8.0 %reshape.421 = f32[32,128,257]{2,1,0:T(8,128)} reshape(f32[32,32896]{1,0:T(8,128)} %concatenate.36) | data formatting | bytes 8421376 | tf_op jit(solution)/shard_map/while/body/eval_jaxpr/reshape | solution.py:60
  260.8 8.0 %reshape.421 = f32[32,128,257]{2,1,0:T(8,128)} reshape(f32[32,32896]{1,0:T(8,128)} %concatenate.36) | data formatting | bytes 8421376 | tf_op jit(solution)/shard_map/while/body/eval_jaxpr/reshape | solution.py:60
  290.3 8.0 %reshape.421 = f32[32,128,257]{2,1,0:T(8,128)} reshape(f32[32,32896]{1,0:T(8,128)} %concatenate.36) | data formatting | bytes 8421376 | tf_op jit(solution)/shard_map/while/body/eval_jaxpr/reshape | solution.py:60
  309.9 5.4 copy.45
  319.9 8.0 %reshape.421 = f32[32,128,257]{2,1,0:T(8,128)} reshape(f32[32,32896]{1,0:T(8,128)} %concatenate.36) | data formatting | bytes 8421376 | tf_op jit(solution)/shard_map/while/body/eval_jaxpr/reshape | solution.py:60
  349.4 8.0 %reshape.421 = f32[32,128,257]{2,1,0:T(8,128)} reshape(f32[32,32896]{1,0:T(8,128)} %concatenate.36) | data formatting | bytes 8421376 | tf_op jit(solution)/shard_map/while/body/eval_jaxpr/reshape | solution.py:60
  379.0 8.0 %reshape.421 = f32[32,128,257]{2,1,0:T(8,128)} reshape(f32[32,32896]{1,0:T(8,128)} %concatenate.36) | data formatting | bytes 8421376 | tf_op jit(solution)/shard_map/while/body/eval_jaxpr/reshape | solution.py:60
  408.5 8.0 %reshape.421 = f32[32,128,257]{2,1,0:T(8,128)} reshape(f32[32,32896]{1,0:T(8,128)} %concatenate.36) | data formatting | bytes 8421376 | tf_op jit(solution)/shard_map/while/body/eval_jaxpr/reshape | solution.py:60
  438.0 8.0 %reshape.421 = f32[32,128,257]{2,1,0:T(8,128)} reshape(f32[32,32896]{1,0:T(8,128)} %concatenate.36) | data formatting | bytes 8421376 | tf_op jit(solution)/shard_map/while/body/eval_jaxpr/reshape | solution.py:60
  467.6 8.0 %reshape.421 = f32[32,128,257]{2,1,0:T(8,128)} reshape(f32[32,32896]{1,0:T(8,128)} %concatenate.36) | data formatting | bytes 8421376 | tf_op jit(solution)/shard_map/while/body/eval_jaxpr/reshape | solution.py:60
  497.1 8.0 %reshape.421 = f32[32,128,257]{2,1,0:T(8,128)} reshape(f32[32,32896]{1,0:T(8,128)} %concatenate.36) | data formatting | bytes 8421376 | tf_op jit(solution)/shard_map/while/body/eval_jaxpr/reshape | solution.py:60
  526.7 8.0 %reshape.421 = f32[32,128,257]{2,1,0:T(8,128)} reshape(f32[32,32896]{1,0:T(8,128)} %concatenate.36) | data formatting | bytes 8421376 | tf_op jit(solution)/shard_map/while/body/eval_jaxpr/reshape | solution.py:60
  552.2 6.2 %all-to-all-done.3 = f32[2,32,32]{2,0,1:T(2,128)S(1)} async-done(((f32[2,32,32]{2,0,1:T(2,128)}), f32[2,32,32]{2,0,1:T(2,128)S(1)}, u32[]{:S(2)}, u32[]{:S(2)}) %all-to-all-start.3) | async-done | bytes 8224 | tf_op jit(solution)/shard_map/all_to_all | solution.py:174
  563.1 24.1 %all-to-all-done.2 = f32[2,32,32,128]{3,2,0,1:T(8,128)S(1)} async-done(((f32[2,32,32,128]{3,2,0,1:T(8,128)}), f32[2,32,32,128]{3,2,0,1:T(8,128)S(1)}, u32[]{:S(2)}, u32[]{:S(2)}) %all-to-all-start.2) | async-done | bytes 1048608 | tf_op jit(solution)/shard_map/all_to_all | solution.py:167
  (378 shorter events, 373.4 us)
Async XLA Ops:
  0.6 0.8 copy-start
  0.6 31.0 %copy-start.2 = (f32[256,128]{1,0:T(8,128)S(1)}, f32[256,128]{1,0:T(8,128)}, u32[]{:S(2)}) copy-start(f32[256,128]{1,0:T(8,128)} %param.23) | copy-start | bytes 393220
  0.7 31.6 %copy-start.1 = (f32[128,128]{1,0:T(8,128)S(1)}, f32[128,128]{1,0:T(8,128)}, u32[]{:S(2)}) copy-start(f32[128,128]{1,0:T(8,128)} %param.22) | copy-start | bytes 196612
  33.8 31.2 %copy-start.3 = (f32[4,128]{1,0:T(4,128)S(1)}, f32[4,128]{1,0:T(4,128)}, u32[]{:S(2)}) copy-start(f32[4,128]{1,0:T(4,128)} %param.21) | copy-start | bytes 6148
  33.8 31.2 %copy-start.4 = (s32[512]{0:T(512)S(1)}, s32[512]{0:T(512)}, u32[]{:S(2)}) copy-start(s32[512]{0:T(512)} %param.15) | copy-start | bytes 6148
  33.8 29.0 %all-to-all-start.1 = ((f32[2,32,32,128]{3,2,0,1:T(8,128)}), f32[2,32,32,128]{3,2,0,1:T(8,128)S(1)}, u32[]{:S(2)}, u32[]{:S(2)}) async-start(f32[2,32,32,128]{3,2,0,1:T(8,128)} %pad_maximum_fusion.1), calls=%async_computation.1 | async-start | bytes 2097152 | tf_op jit(solution)/shard_map/all_to_all | solution.py:91
  547.5 10.8 %all-to-all-start.3 = ((f32[2,32,32]{2,0,1:T(2,128)}), f32[2,32,32]{2,0,1:T(2,128)S(1)}, u32[]{:S(2)}, u32[]{:S(2)}) async-start(f32[2,32,32]{2,0,1:T(2,128)} %pad_maximum_fusion.3), calls=%async_computation.3 | async-start | bytes 65536 | tf_op jit(solution)/shard_map/all_to_all | solution.py:174
  558.3 28.9 %all-to-all-start.2 = ((f32[2,32,32,128]{3,2,0,1:T(8,128)}), f32[2,32,32,128]{3,2,0,1:T(8,128)S(1)}, u32[]{:S(2)}, u32[]{:S(2)}) async-start(f32[2,32,32,128]{3,2,0,1:T(8,128)} %pad_maximum_fusion.2), calls=%async_computation.2 | async-start | bytes 2097152 | tf_op jit(solution)/shard_map/all_to_all | solution.py:167
where the time goes:
time: 595 us; the launch traced here: 590 us
  local copies, waits for them, and re-layouts  314 us (53%)
  other arithmetic  134 us (23%)
  matrix products  59.7 us (10%)
  waiting for transfers between devices  55.6 us (9%)
  blocking collectives  14.4 us (2%)
  starting transfers between devices  9.14 us (2%)
    reshape x16, local copies, waits for them, and re-layouts, diagonal_sums(): skewed = padded.reshape(row_count, tap_count, 2 * tap_count + 1)  128 us
    while x48, local copies, waits for them, and re-layouts  88.2 us
    concatenate x16, local copies, waits for them, and re-layouts, diagonal_sums(): jnp.concatenate([joined, jnp.zeros((row_count, tap_count), jnp.float32)],...  71.9 us
    reduce_sum x16, other arithmetic, diagonal_sums(): column_sums = jnp.sum(skewed, axis=1)  52.8 us
    concatenate x16, other arithmetic, diagonal_sums(): jnp.concatenate([cross_before, cross_now], axis=2)  39.1 us
    all_to_all x1, waiting for transfers between devices, body(): lax.all_to_all(values, ('shot', 'line'), split_axis=1, concat_axis=1, til...  25.3 us
    all_to_all x1, waiting for transfers between devices, body(): lax.all_to_all(send_grad.reshape(2, device_count, slot_cap, tap_count), (...  24.1 us
    reduce_sum x16, other arithmetic, one_block(): jnp.sum(jnp.square(trace_block.astype(jnp.float32)), axis=(1, 2))  16.6 us
  transfers between devices with their start and end apart: 3, of which 3 were waited for; matrix products, arithmetic and copies ran while one was open for 1% of the time, Pallas kernels for 0%

commit v1 on v0

v1 whole, which is shorter than its diff:
```python
import functools

import jax
import jax.numpy as jnp
import numpy as np
from jax import lax
from jax.experimental import pallas as pl
from jax.experimental.pallas import tpu as pltpu
from jax.sharding import PartitionSpec as P

STEP = 0.5
BF = jnp.bfloat16
F32 = jnp.float32
AXES = ("shot", "line")
ROWS = 64
VMEM_LIMIT = 48 * 1024 * 1024


def halves(matrix):
    high = matrix.astype(jnp.bfloat16)
    low = (matrix - high.astype(np.float64)).astype(jnp.bfloat16)
    return high, low


def spectral_tables(taps):
    span = 2 * taps
    theta = 2 * np.pi * (np.arange(taps) + 0.5) / span
    angle = np.arange(span)[:, None] * theta[None, :]
    forward = np.concatenate([np.cos(angle), -np.sin(angle)], axis=1)
    inverse = forward.T / taps
    even = 2 * np.cos(angle[:taps])
    even[0] = 1.0
    fwd_high, fwd_low = halves(forward[:taps])
    twice = np.concatenate([fwd_high, fwd_low], axis=0)

    def triple(matrix):
        high, low = halves(matrix)
        return np.concatenate([high, high, low], axis=0)

    return (
        twice,
        triple(inverse[:, :taps] @ even),
        triple(inverse[:, taps:] @ forward[taps:]),
        triple(inverse[:, :taps]),
    )


def mm(left, right):
    return jnp.dot(left, right, preferred_element_type=F32)


def mm_t(left, right):
    return lax.dot_general(left, right, (((0,), (0,)), ((), ())), preferred_element_type=F32)


def split3(value):
    high = value.astype(BF)
    rest = value - high.astype(F32)
    middle = rest.astype(BF)
    low = (rest - middle.astype(F32)).astype(BF)
    return high, middle, low


def exact_mm(onehot, value):
    high, middle, low = split3(value)
    return mm(onehot, high) + mm(onehot, middle) + mm(onehot, low)


def fine_mm(value, table):
    high = value.astype(BF)
    low = (value - high.astype(F32)).astype(BF)
    return mm(jnp.concatenate([high, low, high], axis=1), table)


def iota(shape, dim):
    return lax.broadcasted_iota(jnp.int32, shape, dim)


def pick_mask(condition):
    return jnp.where(condition, 1.0, 0.0).astype(BF)


def row_to_lanes(row):
    return jnp.transpose(jnp.broadcast_to(row, (128, row.shape[1])))


def find_slots(term_row, home, terms_dev, slot_cap):
    count = term_row.shape[1]
    shift = terms_dev.bit_length() - 1
    lane = iota((count, 128), 1)
    term = row_to_lanes(term_row)
    chunks = home.shape[0]
    high_term, low_term = term >> 7, term & 127
    if chunks <= 128:
        onehot = pick_mask(lane[:, :chunks] == high_term[:, :chunks])
    else:
        onehot = jnp.concatenate(
            [pick_mask(lane + base == high_term) for base in range(0, chunks, 128)], axis=1
        )
    ones = jnp.ones((128, 128), BF)
    here = lane == low_term
    high = mm(onehot, (home >> 7).astype(F32).astype(BF))
    low = mm(onehot, (home & 127).astype(F32).astype(BF))
    high = mm(jnp.where(here, high, 0.0).astype(BF), ones)
    low = mm(jnp.where(here, low, 0.0).astype(BF), ones)
    row = high.astype(jnp.int32) * 128 + low.astype(jnp.int32)
    owner = row >> shift
    place = (row & (terms_dev - 1)).astype(F32)
    owner_hot = pick_mask(lane == owner)
    earlier = pick_mask(iota((count, count), 1) < iota((count, count), 0))
    before = mm(earlier, owner_hot)
    rank = mm(jnp.where(lane == owner, before, 0.0).astype(BF), ones).astype(jnp.int32)
    rank_hot = lane == rank
    request = mm_t(owner_hot, jnp.where(rank_hot, place, 0.0).astype(BF))
    return owner_hot, rank_hot, owner * slot_cap + rank, request


def spread_rows(rows, slot_cap):
    device_count = rows.shape[0]
    slots = device_count * slot_cap
    shift = slot_cap.bit_length() - 1
    where = pick_mask((iota((device_count, slots), 1) >> shift) == iota((device_count, slots), 0))
    high, middle, low = split3(rows)
    wide = mm_t(high, where) + mm_t(middle, where) + mm_t(low, where)
    mine = (iota((128, slots), 1) & (slot_cap - 1)) == iota((128, slots), 0)
    return jnp.sum(jnp.where(mine, wide, 0.0), axis=0, keepdims=True)


def spread_cols(rows, slot_cap):
    device_count = rows.shape[0]
    slots = device_count * slot_cap
    shift = slot_cap.bit_length() - 1
    where = pick_mask((iota((slots, device_count), 0) >> shift) == iota((slots, device_count), 1))
    wide = mm(where, rows.astype(BF))
    mine = (iota((slots, 128), 0) & (slot_cap - 1)) == iota((slots, 128), 1)
    return mm(jnp.where(mine, wide, 0.0).astype(BF), jnp.ones((128, 128), BF))


def lookup(request, filters, slot_cap):
    place = spread_cols(request, slot_cap).astype(jnp.int32)
    lane = iota(place.shape, 1)
    onehot = jnp.concatenate(
        [pick_mask(lane + base == place) for base in range(0, filters.shape[0], 128)], axis=1
    )
    return exact_mm(onehot, filters)


def spectra_rows(trace_rows, target_rows, twice, even, spec_x, spec_t):
    taps = twice.shape[0] // 2
    rows, samples = trace_rows.shape
    blocks = samples // taps

    def stacked(value):
        tall = jnp.concatenate([value[:, b * taps : (b + 1) * taps] for b in range(blocks)], axis=0)
        return jnp.concatenate([tall, tall], axis=1)

    spec_x[...] = mm(stacked(trace_rows), twice)
    spec_t[...] = mm(stacked(target_rows), twice)
    sign = 1.0 - 2.0 * (iota((16, taps), 1) & 1).astype(F32)
    out = []
    for start in range(0, rows, 16):
        c0r = c0i = c1r = c1i = p0 = p1r = p1i = jnp.zeros((16, taps), F32)
        xr0 = xi0 = None
        for b in range(blocks):
            here = pl.ds(b * rows + start, 16)
            xr, xi = spec_x[here, :taps], spec_x[here, taps:]
            tr, ti = spec_t[here, :taps], spec_t[here, taps:]
            c0r += xr * tr + xi * ti
            c0i += xr * ti - xi * tr
            p0 += xr * xr + xi * xi
            if b:
                c1r += xr0 * tr + xi0 * ti
                c1i += xr0 * ti - xi0 * tr
                p1r += xr0 * xr + xi0 * xi
                p1i += xr0 * xi - xi0 * xr
            xr0, xi0 = xr, xi
        power = jnp.sum(p0, axis=1, keepdims=True) * (1.0 / taps)
        out.append(
            (
                jnp.concatenate([p0 + sign * p1i, -sign * p1r], axis=1),
                jnp.concatenate([c0r + sign * c1i, c0i - sign * c1r], axis=1),
                jnp.concatenate([xr0, xi0], axis=1),
                jnp.broadcast_to(power, (16, 128)),
            )
        )
    auto, cross, last, power = (jnp.concatenate(parts, axis=0) for parts in zip(*out))
    return fine_mm(auto, even), cross, last, power


def gradients(mixed, q, cross, last, twice, tail, inverse):
    taps = q.shape[1]
    fs = mm(jnp.concatenate([mixed, mixed], axis=1), twice)
    fr, fi = fs[:, :taps], fs[:, taps:]
    xr, xi = last[:, :taps], last[:, taps:]
    over = fine_mm(jnp.concatenate([xr * fr - xi * fi, xr * fi + xi * fr], axis=1), tail)
    yr, yi = over[:, :taps], over[:, taps:]
    gr = q * fr - cross[:, :taps] - (xr * yr + xi * yi)
    gi = q * fi - cross[:, taps:] - (xr * yi - xi * yr)
    return fine_mm(jnp.concatenate([gr, gi], axis=1), inverse)


def slot_hot(slot, slots):
    lane = iota(slot.shape, 1)
    return jnp.concatenate([pick_mask(lane + base == slot) for base in range(0, slots, 128)], axis=1)


def slot_hot_t(slot, slots):
    row = jnp.transpose(slot)[0:1, :]
    return pick_mask(iota((slots, slot.shape[0]), 0) == row)


def settled(filters, place_row, grad_in, power_row):
    terms = filters.shape[0]
    here = iota((terms, place_row.shape[1]), 0) == place_row.astype(jnp.int32)
    sums = exact_mm(pick_mask(here), grad_in)
    energy = jnp.sum(jnp.where(here, power_row, 0.0), axis=1, keepdims=True)
    return filters - STEP * sums / jnp.maximum(energy, 1.0)


def settled_src(filters, src_row, grads, power):
    terms = filters.shape[0]
    here = pick_mask(iota((8, src_row.shape[1]), 0) == src_row)
    sums = exact_mm(here, grads)[:terms]
    energy = exact_mm(here, power)[:terms]
    return filters - STEP * sums / jnp.maximum(energy, 1.0)


def src_rows(src_row, src_filters):
    here = pick_mask(iota((8, src_row.shape[1]), 0) == src_row)
    high, middle, low = split3(
        jnp.concatenate([src_filters, jnp.zeros((8 - src_filters.shape[0], src_filters.shape[1]), F32)], axis=0)
    )
    return mm_t(here, high) + mm_t(here, middle) + mm_t(here, low)


def index_kernel(device_count, slot_cap, terms, rcv_t, cmp_t, rcv_h, cmp_h, slots, ranks, request):
    for table, (term, home) in enumerate(((rcv_t, rcv_h), (cmp_t, cmp_h))):
        owner_hot, rank_hot, slot, req = find_slots(term[...], home[...], terms[table], slot_cap)
        slots[table] = slot
        request[table] = req[:device_count]


def lookup_kernel(slot_cap, request, rcv, cmp, out):
    out[0] = lookup(request[0], rcv[...], slot_cap)
    out[1] = lookup(request[1], cmp[...], slot_cap)


def spectra_kernel(traces, targets, twice, even, q, cross, last, power, spec_x, spec_t):
    q[...], cross[...], last[...], power[...] = spectra_rows(
        traces[...], targets[...], twice[...], even[...], spec_x, spec_t
    )


def post_kernel(
    device_count, slot_cap, counts, src_row, src_filters, slots, fetched, q, cross, last, power,
    twice, tail, inverse, src_out, send, send_power,
):
    total = device_count * slot_cap
    count = q.shape[0]
    mixed = src_rows(src_row[...], src_filters[...])
    for table in range(2):
        mixed = mixed + exact_mm(slot_hot(slots[table], total), fetched[table])
    grads = gradients(mixed.astype(BF), q[...], cross[...], last[...], twice[...], tail[...], inverse[...])
    live = iota((count, 128), 0) < counts[0]
    grads = jnp.where(live, grads, 0.0)
    powers = jnp.where(live, power[...], 0.0)
    src_out[...] = settled_src(src_filters[...], src_row[...], grads, powers)
    for table in range(2):
        slot = slots[table]
        send[table] = exact_mm(slot_hot_t(slot, total), grads)
        shift = slot_cap.bit_length() - 1
        lane = iota((count, 128), 1)
        owner_hot = pick_mask(lane == slot >> shift)
        high, middle, low = split3(jnp.where(lane == (slot & (slot_cap - 1)), powers, 0.0))
        sent = mm_t(owner_hot, high) + mm_t(owner_hot, middle) + mm_t(owner_hot, low)
        send_power[table] = sent[:device_count]


def settle_kernel(slot_cap, request, got, got_power, rcv, cmp, rcv_out, cmp_out):
    for table, (filters, out) in enumerate(((rcv, rcv_out), (cmp, cmp_out))):
        place_row = spread_rows(request[table], slot_cap)
        power_row = spread_rows(got_power[table], slot_cap)
        out[...] = settled(filters[...], place_row, got[table], power_row)


def call(kernel, outs, cost=None, **kwargs):
    return pl.pallas_call(
        kernel,
        out_shape=outs,
        compiler_params=pltpu.CompilerParams(vmem_limit_bytes=VMEM_LIMIT),
        cost_estimate=cost,
        **kwargs,
    )


def exchange(value):
    return lax.all_to_all(value, AXES, split_axis=1, concat_axis=1, tiled=True)


def body(
    traces, targets, src_local, rcv_term, cmp_term, rcv_home, cmp_home, counts,
    src_filters, rcv_filters, cmp_filters,
):
    trace_rows, samples = traces.shape
    taps = src_filters.shape[1]
    device_count = lax.axis_size(AXES)
    slot_cap = max(2, 2 * trace_rows // device_count)
    total = device_count * slot_cap
    blocks = samples // taps
    terms = (rcv_filters.shape[0], cmp_filters.shape[0])
    twice, even, tail, inverse = (jnp.asarray(table) for table in spectral_tables(taps))
    shape = jax.ShapeDtypeStruct
    src_row = src_local.reshape(1, -1)

    slots, request = call(
        lambda a, b, c, d, s, r: index_kernel(device_count, slot_cap, terms, a, b, c, d, s, None, r),
        (shape((2, trace_rows, 128), jnp.int32), shape((2, device_count, 128), F32)),
    )(
        rcv_term.reshape(1, -1), cmp_term.reshape(1, -1),
        rcv_home.reshape(-1, 128), cmp_home.reshape(-1, 128),
    )
    received = exchange(request)
    values = call(
        functools.partial(lookup_kernel, slot_cap), shape((2, total, taps), F32)
    )(received, rcv_filters, cmp_filters)
    fetched = exchange(values.reshape(2, device_count, slot_cap, taps)).reshape(2, total, taps)

    whole = lambda i: (0, 0)
    block = lambda width: pl.BlockSpec((ROWS, width), lambda i: (i, 0))
    q, cross, last, power = call(
        spectra_kernel,
        tuple(shape((trace_rows, width), F32) for width in (taps, 2 * taps, 2 * taps, 128)),
        cost=pl.CostEstimate(flops=4 * trace_rows * samples * 4 * taps, bytes_accessed=6 * 2**20, transcendentals=0),
        grid=(trace_rows // ROWS,),
        in_specs=[block(samples), block(samples), pl.BlockSpec(twice.shape, whole), pl.BlockSpec(even.shape, whole)],
        out_specs=tuple(block(width) for width in (taps, 2 * taps, 2 * taps, 128)),
        scratch_shapes=[pltpu.VMEM((ROWS * blocks, 2 * taps), F32)] * 2,
    )(traces, targets, twice, even)

    smem = pl.BlockSpec(memory_space=pltpu.SMEM)
    vmem = pl.BlockSpec(memory_space=pltpu.VMEM)
    src_out, send, send_power = call(
        functools.partial(post_kernel, device_count, slot_cap),
        (
            shape(src_filters.shape, F32),
            shape((2, total, taps), F32),
            shape((2, device_count, 128), F32),
        ),
        in_specs=[smem] + [vmem] * 11,
    )(counts, src_row, src_filters, slots, fetched, q, cross, last, power, twice, tail, inverse)
    got = exchange(send.reshape(2, device_count, slot_cap, taps)).reshape(2, total, taps)
    got_power = exchange(send_power)
    rcv_out, cmp_out = call(
        functools.partial(settle_kernel, slot_cap),
        (shape(rcv_filters.shape, F32), shape(cmp_filters.shape, F32)),
    )(received, got, got_power, rcv_filters, cmp_filters)
    return src_out, rcv_out, cmp_out


def solution(mesh):
    rows, flat = P(AXES, None), P(AXES)
    return jax.shard_map(
        body,
        mesh=mesh,
        in_specs=(rows, rows, flat, flat, flat, P(), P(), flat, rows, rows, rows),
        out_specs=(rows, rows, rows),
        check_vma=False,
    )
```

time: 595 us -> 104 us (0.17)
  local copies, waits for them, and re-layouts: 314 us -> 12.8 us
  other arithmetic: 134 us -> 0 us
  matrix products: 59.7 us -> 0 us
  Pallas kernels: 0 us -> 17.5 us
  waiting for transfers between devices: 55.6 us -> 47.4 us
    reshape x16 -> x2, local copies, waits for them, and re-layouts: 128 us -> 2.16 us  [the longest x1 1.11 us: body(): send.reshape(2, device_count, slot_cap, taps)]
    while x48 -> x0, local copies, waits for them, and re-layouts: 88.2 us -> none
    concatenate x16 -> x0, local copies, waits for them, and re-layouts: 71.9 us -> none  [diagonal_sums(): jnp.concatenate([joined, jnp.zeros((row_count, tap_count), jnp.float32)],...]
    reduce_sum x34 -> x0, other arithmetic: 69.6 us -> none  [the longest x16 52.8 us: diagonal_sums(): column_sums = jnp.sum(skewed, axis=1)]
    dot_general x105 -> x0, matrix products: 59.7 us -> none  [the longest x16 11.2 us: one_block(): jnp.einsum('rk,kji->rji', filter_block, shift_upper, preferred_element_ty...]
    concatenate x16 -> x0, other arithmetic: 39.1 us -> none  [diagonal_sums(): jnp.concatenate([cross_before, cross_now], axis=2)]
    pallas_call x0 -> x5, Pallas kernels: none -> 17.5 us  [the longest x1 6.59 us: body(): call(spectra_kernel, tuple((shape((trace_rows, width), F32) for width in...]
    while x16 -> x0, other arithmetic: 15.9 us -> none
  transfers between devices with their start and end apart: 3 -> 3, of which waited for: 3 -> 3; matrix products, arithmetic and copies ran while one was open for 1% -> 1% of each run, Pallas kernels for 0% -> 6%
where the time goes in v1:
time: 104 us; the launch traced here: 103 us
  waiting for transfers between devices  47.4 us (46%)
  Pallas kernels  17.5 us (17%)
  blocking collectives  14.4 us (14%)
  local copies, waits for them, and re-layouts  12.8 us (12%)
  starting transfers between devices  9.56 us (9%)
  between operations  1.49 us (1%)
    all_to_all x3, waiting for transfers between devices, exchange(): return lax.all_to_all(value, AXES, split_axis=1, concat_axis=1, tiled=True)  47.4 us
    all_to_all x1, blocking collectives, exchange(): return lax.all_to_all(value, AXES, split_axis=1, concat_axis=1, tiled=True)  14.4 us
    all_to_all x3, starting transfers between devices, exchange(): return lax.all_to_all(value, AXES, split_axis=1, concat_axis=1, tiled=True)  9.56 us
    unnamed x38, local copies, waits for them, and re-layouts  8.49 us
    pallas_call x1, Pallas kernels, body(): call(spectra_kernel, tuple((shape((trace_rows, width), F32) for width in...  6.59 us
    pallas_call x1, Pallas kernels, body(): call(functools.partial(post_kernel, device_count, slot_cap), (shape(src_f...  5.12 us
    pallas_call x1, Pallas kernels, body(): call(functools.partial(settle_kernel, slot_cap), (shape(rcv_filters.shape...  2.54 us
  transfers between devices with their start and end apart: 3, of which 3 were waited for; matrix products, arithmetic and copies ran while one was open for 1% of the time, Pallas kernels for 6%

profile of v1, /device:TPU:0, one launch (start us, length us, event | category | flops | bytes accessed | tf_op | source)
XLA Modules:
  0.0 103.0 jit_solution(10795065917449598812)
XLA Ops:
  0.6 0.7 copy-done.10
  1.4 0.7 copy-done.11
  2.1 0.7 copy-done.14
  2.8 0.7 copy-done.15
  3.5 2.0 %shard_map.166 = (s32[2,512,128]{2,1,0:T(8,128)S(1)}, f32[2,32,128]{2,1,0:T(8,128)S(1)}) custom-call(s32[1,512]{1,0:T(1,128)S(1)} %bitcast.16, s32[1,512]{1,0:T(1,128)S(1)} %bitcast.17, s32[32,128]{1,0:T(8,128)S(1)} %bitcast.14, s32[64,128]{1,0:T(8,128)S(1)} %bitcast.13), custom_call_target="tpu_custom_call" | custom-call | tf_op jit(solution)/shard_map/pallas_call | solution.py:315
  5.6 14.4 %all_to_all.20 = f32[2,32,128]{2,0,1:T(2,128)S(1)} all-to-all(f32[2,32,128]{2,0,1:T(2,128)S(1)} %copy.18), channel_id=1, replica_groups=mesh['shot'=8,'line'=4] {'shot','line'}, dimensions={1} | all-to-all | bytes 65536 | tf_op jit(solution)/shard_map/all_to_all | solution.py:297
  19.9 0.9 copy-done
  20.8 0.8 copy-done.5
  21.7 1.2 %shard_map.167 = f32[2,1024,128]{2,1,0:T(8,128)S(1)} custom-call(f32[2,32,128]{2,1,0:T(8,128)S(1)} %copy.19.request, f32[128,128]{1,0:T(8,128)S(1)} %copy-done.5, f32[256,128]{1,0:T(8,128)S(1)} %copy-done), custom_call_target="tpu_custom_call" | custom-call | tf_op jit(solution)/shard_map/pallas_call | solution.py:323
  22.9 1.1 %copy.20 = f32[2,32,32,128]{3,2,0,1:T(8,128)} copy(f32[2,32,32,128]{3,2,1,0:T(8,128)S(1)} %bitcast.11) | data formatting | bytes 2097152 | tf_op jit(solution)/shard_map/reshape | solution.py:326
  23.9 3.4 %all-to-all-start.1 = ((f32[2,32,32,128]{3,2,0,1:T(8,128)}), f32[2,32,32,128]{3,2,0,1:T(8,128)}, u32[]{:S(2)}, u32[]{:S(2)}) async-start(f32[2,32,32,128]{3,2,0,1:T(8,128)} %copy.20), calls=%async_computation.1 | async-start | bytes 2097152 | tf_op jit(solution)/shard_map/all_to_all | solution.py:297
  28.0 1.6 %copy-done.16 = bf16[512,2048]{1,0:T(8,128)(2,1)S(1)} copy-done((bf16[512,2048]{1,0:T(8,128)(2,1)S(1)}, bf16[512,2048]{1,0:T(8,128)(2,1)}, u32[]{:S(2)}) %copy-start.16) | copy-done | bytes 2097176
  29.6 1.6 %copy-done.17 = bf16[512,2048]{1,0:T(8,128)(2,1)S(1)} copy-done((bf16[512,2048]{1,0:T(8,128)(2,1)S(1)}, bf16[512,2048]{1,0:T(8,128)(2,1)}, u32[]{:S(2)}) %copy-start.17) | copy-done | bytes 2097176
  31.2 6.6 %shard_map.168 = (f32[512,128]{1,0:T(8,128)S(1)}, f32[512,256]{1,0:T(8,128)S(1)}, f32[512,256]{1,0:T(8,128)S(1)}, f32[512,128]{1,0:T(8,128)S(1)}) custom-call(bf16[512,2048]{1,0:T(8,128)(2,1)S(1)} %copy-done.16, bf16[512,2048]{1,0:T(8,128)(2,1)S(1)} %copy-done.17, bf16[256,256]{1,0:T(8,128)(2,1)S(1)} %copy-done.8, bf16[768,128]{1,0:T(8,128)(2,1)S(1)} %copy-done.18), custom_call_target="tpu_custom_call" | custom-call | flops 2147483648 | bytes 6291456 | tf_op jit(solution)/shard_map/pallas_call | solution.py:330
  37.8 0.7 copy-done.3
  38.5 15.0 %all-to-all-done.1 = f32[2,32,32,128]{3,2,0,1:T(8,128)} async-done(((f32[2,32,32,128]{3,2,0,1:T(8,128)}), f32[2,32,32,128]{3,2,0,1:T(8,128)}, u32[]{:S(2)}, u32[]{:S(2)}) %all-to-all-start.1) | async-done | bytes 1048608 | tf_op jit(solution)/shard_map/all_to_all | solution.py:297
  53.5 1.3 %copy.21 = f32[2,32,32,128]{3,2,1,0:T(8,128)S(1)} copy(f32[2,32,32,128]{3,2,0,1:T(8,128)} %all-to-all-done.1) | data formatting | bytes 2097152 | tf_op jit(solution)/shard_map/all_to_all | solution.py:297
  54.9 5.1 %shard_map.169 = (f32[4,128]{1,0:T(4,128)}, f32[2,1024,128]{2,1,0:T(8,128)S(1)}, f32[2,32,128]{2,1,0:T(8,128)S(1)}) custom-call(s32[1]{0:T(128)S(6)} %copy.27.counts, s32[1,512]{1,0:T(1,128)S(1)} %bitcast.15, f32[4,128]{1,0:T(4,128)S(1)} %copy-done.13, s32[2,512,128]{2,1,0:T(8,128)S(1)} %get-tuple-element.14.slots, f32[2,1024,128]{2,1,0:T(8,128)S(1)} %bitcast.9, ...), custom_call_target="tpu_custom_call" | custom-call | tf_op jit(solution)/shard_map/pallas_call | solution.py:342
  60.7 3.5 %all-to-all-start.3 = ((f32[2,32,128]{2,0,1:T(2,128)}), f32[2,32,128]{2,0,1:T(2,128)S(1)}, u32[]{:S(2)}, u32[]{:S(2)}) async-start(f32[2,32,128]{2,0,1:T(2,128)} %copy.24), calls=%async_computation.3 | async-start | bytes 65536 | tf_op jit(solution)/shard_map/all_to_all | solution.py:297
  64.3 1.1 %copy.22 = f32[2,32,32,128]{3,2,0,1:T(8,128)} copy(f32[2,32,32,128]{3,2,1,0:T(8,128)S(1)} %bitcast.12) | data formatting | bytes 2097152 | tf_op jit(solution)/shard_map/reshape | solution.py:351
  65.4 6.1 %all-to-all-done.3 = f32[2,32,128]{2,0,1:T(2,128)S(1)} async-done(((f32[2,32,128]{2,0,1:T(2,128)}), f32[2,32,128]{2,0,1:T(2,128)S(1)}, u32[]{:S(2)}, u32[]{:S(2)}) %all-to-all-start.3) | async-done | bytes 32800 | tf_op jit(solution)/shard_map/all_to_all | solution.py:297
  71.5 2.6 %all-to-all-start.2 = ((f32[2,32,32,128]{3,2,0,1:T(8,128)}), f32[2,32,32,128]{3,2,0,1:T(8,128)S(1)}, u32[]{:S(2)}, u32[]{:S(2)}) async-start(f32[2,32,32,128]{3,2,0,1:T(8,128)} %copy.22), calls=%async_computation.2 | async-start | bytes 2097152 | tf_op jit(solution)/shard_map/all_to_all | solution.py:297
  74.2 26.2 %all-to-all-done.2 = f32[2,32,32,128]{3,2,0,1:T(8,128)S(1)} async-done(((f32[2,32,32,128]{3,2,0,1:T(8,128)}), f32[2,32,32,128]{3,2,0,1:T(8,128)S(1)}, u32[]{:S(2)}, u32[]{:S(2)}) %all-to-all-start.2) | async-done | bytes 1048608 | tf_op jit(solution)/shard_map/all_to_all | solution.py:297
  100.5 2.5 %shard_map.170 = (f32[128,128]{1,0:T(8,128)}, f32[256,128]{1,0:T(8,128)}) custom-call(f32[2,32,128]{2,1,0:T(8,128)S(1)} %copy.19.request, f32[2,1024,128]{2,1,0:T(8,128)S(1)} %bitcast.10, f32[2,32,128]{2,1,0:T(8,128)S(1)} %copy.26.got_power, f32[128,128]{1,0:T(8,128)S(1)} %copy-done.6, f32[256,128]{1,0:T(8,128)S(1)} %copy-done.1), custom_call_target="tpu_custom_call" | custom-call | tf_op jit(solution)/shard_map/pallas_call | solution.py:353
  (34 shorter events, 0.8 us)
Async XLA Ops:
  0.6 0.8 copy-start.10
  1.4 0.7 copy-start.11
  2.1 0.7 copy-start.14
  2.8 0.7 copy-start.15
  19.9 0.9 copy-start
  20.8 0.8 copy-start.5
  22.9 5.1 %copy-start.8 = (bf16[256,256]{1,0:T(8,128)(2,1)S(1)}, bf16[256,256]{1,0:T(8,128)(2,1)}, u32[]{:S(2)}) copy-start(bf16[256,256]{1,0:T(8,128)(2,1)} %constant.8.clone.twice) | copy-start | bytes 393220
  22.9 5.1 %copy-start.18 = (bf16[768,128]{1,0:T(8,128)(2,1)S(1)}, bf16[768,128]{1,0:T(8,128)(2,1)}, u32[]{:S(2)}) copy-start(bf16[768,128]{1,0:T(8,128)(2,1)} %constant.9.clone.even) | copy-start | bytes 589828
  23.9 29.6 %all-to-all-start.1 = ((f32[2,32,32,128]{3,2,0,1:T(8,128)}), f32[2,32,32,128]{3,2,0,1:T(8,128)}, u32[]{:S(2)}, u32[]{:S(2)}) async-start(f32[2,32,32,128]{3,2,0,1:T(8,128)} %copy.20), calls=%async_computation.1 | async-start | bytes 2097152 | tf_op jit(solution)/shard_map/all_to_all | solution.py:297
  28.0 1.6 %copy-start.16 = (bf16[512,2048]{1,0:T(8,128)(2,1)S(1)}, bf16[512,2048]{1,0:T(8,128)(2,1)}, u32[]{:S(2)}) copy-start(bf16[512,2048]{1,0:T(8,128)(2,1)} %traces.1) | copy-start | bytes 6291460
  29.6 1.6 %copy-start.17 = (bf16[512,2048]{1,0:T(8,128)(2,1)S(1)}, bf16[512,2048]{1,0:T(8,128)(2,1)}, u32[]{:S(2)}) copy-start(bf16[512,2048]{1,0:T(8,128)(2,1)} %targets.1) | copy-start | bytes 6291460
  37.8 0.7 copy-start.3
  38.5 16.4 %copy-start.2 = (bf16[768,256]{1,0:T(8,128)(2,1)S(1)}, bf16[768,256]{1,0:T(8,128)(2,1)}, u32[]{:S(2)}) copy-start(bf16[768,256]{1,0:T(8,128)(2,1)} %constant.10.clone.tail) | copy-start | bytes 1179652
  38.5 16.4 %copy-start.7 = (bf16[768,128]{1,0:T(8,128)(2,1)S(1)}, bf16[768,128]{1,0:T(8,128)(2,1)}, u32[]{:S(2)}) copy-start(bf16[768,128]{1,0:T(8,128)(2,1)} %constant.11.clone.inverse) | copy-start | bytes 589828
  38.5 16.4 %copy-start.12 = (s32[512]{0:T(512)S(1)}, s32[512]{0:T(512)}, u32[]{:S(2)}) copy-start(s32[512]{0:T(512)} %param.17) | copy-start | bytes 6148
  38.5 16.4 %copy-start.13 = (f32[4,128]{1,0:T(4,128)S(1)}, f32[4,128]{1,0:T(4,128)}, u32[]{:S(2)}) copy-start(f32[4,128]{1,0:T(4,128)} %src_filters.1) | copy-start | bytes 6148
  53.5 1.4 %copy-start.4 = (f32[512,128]{1,0:T(8,128)S(1)}, f32[512,128]{1,0:T(8,128)}, u32[]{:S(2)}) copy-start(f32[512,128]{1,0:T(8,128)} %copy-done.3) | copy-start | bytes 786436
  53.5 1.4 %copy-start.9 = (bf16[256,256]{1,0:T(8,128)(2,1)S(1)}, bf16[256,256]{1,0:T(8,128)(2,1)}, u32[]{:S(2)}) copy-start(bf16[256,256]{1,0:T(8,128)(2,1)} %constant.8.clone.twice) | copy-start | bytes 393220
  60.7 10.8 %all-to-all-start.3 = ((f32[2,32,128]{2,0,1:T(2,128)}), f32[2,32,128]{2,0,1:T(2,128)S(1)}, u32[]{:S(2)}, u32[]{:S(2)}) async-start(f32[2,32,128]{2,0,1:T(2,128)} %copy.24), calls=%async_computation.3 | async-start | bytes 65536 | tf_op jit(solution)/shard_map/all_to_all | solution.py:297
  65.4 35.1 %copy-start.1 = (f32[256,128]{1,0:T(8,128)S(1)}, f32[256,128]{1,0:T(8,128)}, u32[]{:S(2)}) copy-start(f32[256,128]{1,0:T(8,128)} %cmp.3) | copy-start | bytes 393220
  65.4 35.1 %copy-start.6 = (f32[128,128]{1,0:T(8,128)S(1)}, f32[128,128]{1,0:T(8,128)}, u32[]{:S(2)}) copy-start(f32[128,128]{1,0:T(8,128)} %rcv.3) | copy-start | bytes 196612
  71.5 28.9 %all-to-all-start.2 = ((f32[2,32,32,128]{3,2,0,1:T(8,128)}), f32[2,32,32,128]{3,2,0,1:T(8,128)S(1)}, u32[]{:S(2)}, u32[]{:S(2)}) async-start(f32[2,32,32,128]{3,2,0,1:T(8,128)} %copy.22), calls=%async_computation.2 | async-start | bytes 2097152 | tf_op jit(solution)/shard_map/all_to_all | solution.py:297

commit v2 on v1

v2 whole, which is shorter than its diff:
```python
import functools

import jax
import jax.numpy as jnp
import numpy as np
from jax import lax
from jax.experimental import pallas as pl
from jax.experimental.pallas import tpu as pltpu
from jax.sharding import PartitionSpec as P

STEP = 0.5
BF = jnp.bfloat16
F32 = jnp.float32
AXES = ("shot", "line")
ROWS = 64
Z = 4
VMEM_LIMIT = 48 * 1024 * 1024


def halves(matrix):
    high = matrix.astype(jnp.bfloat16)
    low = (matrix - high.astype(np.float64)).astype(jnp.bfloat16)
    return high, low


def spectral_tables(taps):
    span = 2 * taps
    theta = 2 * np.pi * (np.arange(taps) + 0.5) / span
    angle = np.arange(span)[:, None] * theta[None, :]
    forward = np.concatenate([np.cos(angle), -np.sin(angle)], axis=1)
    inverse = forward.T / taps
    even = 2 * np.cos(angle[:taps])
    even[0] = 1.0
    fwd_high, fwd_low = halves(forward[:taps])
    twice = np.concatenate([fwd_high, fwd_low], axis=0)

    def triple(matrix):
        high, low = halves(matrix)
        return np.concatenate([high, high, low], axis=0)

    return (
        twice,
        triple(inverse[:, :taps] @ even),
        triple(inverse[:, taps:] @ forward[taps:]),
        triple(inverse[:, :taps]),
    )


def mm(left, right):
    return jnp.dot(left, right, preferred_element_type=F32)


def mm_t(left, right):
    return lax.dot_general(left, right, (((0,), (0,)), ((), ())), preferred_element_type=F32)


def split3(value):
    high = value.astype(BF)
    rest = value - high.astype(F32)
    middle = rest.astype(BF)
    low = (rest - middle.astype(F32)).astype(BF)
    return high, middle, low


def exact_mm(onehot, value):
    high, middle, low = split3(value)
    return mm(onehot, high) + mm(onehot, middle) + mm(onehot, low)


def fine_mm(value, table):
    high = value.astype(BF)
    low = (value - high.astype(F32)).astype(BF)
    return mm(jnp.concatenate([high, low, high], axis=1), table)


def iota(shape, dim):
    return lax.broadcasted_iota(jnp.int32, shape, dim)


def pick_mask(condition):
    return jnp.where(condition, 1.0, 0.0).astype(BF)


def row_to_lanes(row):
    return jnp.transpose(jnp.broadcast_to(row, (128, row.shape[1])))


def find_slots(term_row, home, terms_dev):
    count = term_row.shape[1]
    shift = terms_dev.bit_length() - 1
    lane = iota((count, 128), 1)
    term = row_to_lanes(term_row)
    chunks = home.shape[0]
    high_term, low_term = term >> 7, term & 127
    if chunks <= 128:
        onehot = pick_mask(lane[:, :chunks] == high_term[:, :chunks])
    else:
        onehot = jnp.concatenate(
            [pick_mask(lane + base == high_term) for base in range(0, chunks, 128)], axis=1
        )
    ones = jnp.ones((128, 128), BF)
    here = lane == low_term
    high = mm(onehot, (home >> 7).astype(F32).astype(BF))
    low = mm(onehot, (home & 127).astype(F32).astype(BF))
    high = mm(jnp.where(here, high, 0.0).astype(BF), ones)
    low = mm(jnp.where(here, low, 0.0).astype(BF), ones)
    row = high.astype(jnp.int32) * 128 + low.astype(jnp.int32)
    owner = row >> shift
    place = (row & (terms_dev - 1)).astype(F32)
    earlier = pick_mask(iota((count, count), 1) < iota((count, count), 0))
    before = mm(earlier, pick_mask(lane == owner))
    rank = mm(jnp.where(lane == owner, before, 0.0).astype(BF), ones).astype(jnp.int32)
    return owner, rank, place


def as_row(lanes):
    return jnp.transpose(lanes)[0:1, :]


def both_hot(slots, base, width):
    lane = iota(slots[0].shape, 1)
    parts = []
    for start in range(0, width, 128):
        here = lane + (base + start)
        parts.append(pick_mask((here == slots[0]) | (here == slots[1])))
    return jnp.concatenate(parts, axis=1)


def spectra_rows(trace_rows, target_rows, twice, even, spec_x, spec_t):
    taps = twice.shape[0] // 2
    rows, samples = trace_rows.shape
    blocks = samples // taps

    def stacked(value):
        tall = jnp.concatenate([value[:, b * taps : (b + 1) * taps] for b in range(blocks)], axis=0)
        return jnp.concatenate([tall, tall], axis=1)

    spec_x[...] = mm(stacked(trace_rows), twice)
    spec_t[...] = mm(stacked(target_rows), twice)
    sign = 1.0 - 2.0 * (iota((16, taps), 1) & 1).astype(F32)
    out = []
    for start in range(0, rows, 16):
        c0r = c0i = c1r = c1i = p0 = p1r = p1i = jnp.zeros((16, taps), F32)
        xr0 = xi0 = None
        for b in range(blocks):
            here = pl.ds(b * rows + start, 16)
            xr, xi = spec_x[here, :taps], spec_x[here, taps:]
            tr, ti = spec_t[here, :taps], spec_t[here, taps:]
            c0r += xr * tr + xi * ti
            c0i += xr * ti - xi * tr
            p0 += xr * xr + xi * xi
            if b:
                c1r += xr0 * tr + xi0 * ti
                c1i += xr0 * ti - xi0 * tr
                p1r += xr0 * xr + xi0 * xi
                p1i += xr0 * xi - xi0 * xr
            xr0, xi0 = xr, xi
        power = jnp.sum(p0, axis=1, keepdims=True) * (1.0 / taps)
        out.append(
            (
                jnp.concatenate([p0 + sign * p1i, -sign * p1r], axis=1),
                jnp.concatenate([c0r + sign * c1i, c0i - sign * c1r], axis=1),
                jnp.concatenate([xr0, xi0], axis=1),
                jnp.broadcast_to(power, (16, 128)),
            )
        )
    auto, cross, last, power = (jnp.concatenate(parts, axis=0) for parts in zip(*out))
    return fine_mm(auto, even), cross, last, power


def gradients(mixed, q, cross, last, twice, tail, inverse):
    taps = q.shape[1]
    fs = mm(jnp.concatenate([mixed, mixed], axis=1), twice)
    fr, fi = fs[:, :taps], fs[:, taps:]
    xr, xi = last[:, :taps], last[:, taps:]
    over = fine_mm(jnp.concatenate([xr * fr - xi * fi, xr * fi + xi * fr], axis=1), tail)
    yr, yi = over[:, :taps], over[:, taps:]
    gr = q * fr - cross[:, :taps] - (xr * yr + xi * yi)
    gi = q * fi - cross[:, taps:] - (xr * yi - xi * yr)
    return fine_mm(jnp.concatenate([gr, gi], axis=1), inverse)


def settled_src(filters, src_row, grads, power):
    terms = filters.shape[0]
    here = pick_mask(iota((8, src_row.shape[1]), 0) == src_row)
    sums = exact_mm(here, grads)[:terms]
    energy = exact_mm(here, power)[:terms]
    return filters - STEP * sums / jnp.maximum(energy, 1.0)


def src_rows(src_row, src_filters):
    here = pick_mask(iota((8, src_row.shape[1]), 0) == src_row)
    high, middle, low = split3(
        jnp.concatenate([src_filters, jnp.zeros((8 - src_filters.shape[0], src_filters.shape[1]), F32)], axis=0)
    )
    return mm_t(here, high) + mm_t(here, middle) + mm_t(here, low)


def fused_kernel(
    sizes, counts, traces, targets, src_row, rcv_row, cmp_row, rcv_home, cmp_home,
    src_f, rcv_f, cmp_f, twice, even, tail, inverse,
    src_out, rcv_out, cmp_out,
    v_traces, v_targets, v_src_row, v_rcv_row, v_cmp_row, v_rcv_home, v_cmp_home,
    v_src_f, v_twice, v_even, v_tail, v_inverse,
    table, req_send, req_recv, vals, fetched, hot, grad_send, grad_recv, part, inbox,
    q, cross, last, power, spec_x, spec_t,
    local_sem, req_ss, req_rs, tab_ss, tab_rs, val_ss, val_rs, grad_ss, grad_rs, part_ss, part_rs,
):
    lines, plane, slot_cap, terms = sizes
    rcv_terms, cmp_terms = terms
    rows_all = rcv_terms + cmp_terms
    pair = 2 * slot_cap
    width = plane * pair
    count = v_traces.shape[0]
    me = lax.axis_index("shot") * lines + lax.axis_index("line")
    z, p = me // plane, me % plane

    def device(index):
        return (index // lines, index % lines)

    def peer(offset):
        return (p + offset) % plane

    def remote(source, target, send, recv, index):
        return pltpu.make_async_remote_copy(
            src_ref=source, dst_ref=target, send_sem=send, recv_sem=recv,
            device_id=device(index), device_id_type=pl.DeviceIdType.MESH,
        )

    small = [
        (rcv_row, v_rcv_row), (cmp_row, v_cmp_row), (rcv_home, v_rcv_home), (cmp_home, v_cmp_home),
        (rcv_f, table.at[z, pl.ds(0, rcv_terms)]), (cmp_f, table.at[z, pl.ds(rcv_terms, cmp_terms)]),
        (src_row, v_src_row), (src_f, v_src_f), (twice, v_twice), (even, v_even),
        (tail, v_tail), (inverse, v_inverse), (traces, v_traces), (targets, v_targets),
    ]
    copies = [
        pltpu.make_async_copy(source, target, local_sem.at[i]) for i, (source, target) in enumerate(small)
    ]
    for copy in copies:
        copy.start()
    barrier = pltpu.get_barrier_semaphore()

    def greet(index):
        pl.semaphore_signal(barrier, inc=1, device_id=device(index), device_id_type=pl.DeviceIdType.MESH)

    for offset in range(1, plane):
        greet(z * plane + peer(offset))
    for distance in range(1, Z):
        greet((z + distance) % Z * plane + p)
    pl.semaphore_wait(barrier, plane - 1 + Z - 1)

    def table_copy(way, distance):
        chunk = z - distance if way == 0 else z + distance
        target = me + plane if way == 0 else me - plane
        return remote(
            table.at[chunk], table.at[chunk], tab_ss.at[way, distance], tab_rs.at[way, distance + 1], target
        )

    def table_wait(way, distance):
        chunk = z - distance if way == 0 else z + distance
        remote(
            table.at[chunk], table.at[chunk], tab_ss.at[way, distance], tab_rs.at[way, distance], me
        ).wait_recv()

    def arrives(way, distance):
        return z >= distance if way == 0 else z <= Z - 1 - distance

    def goes_on(way, distance):
        return ((z >= distance) & (z < Z - 1)) if way == 0 else ((z <= Z - 1 - distance) & (z > 0))

    copies[4].wait()
    copies[5].wait()
    for way in range(2):
        pl.when(goes_on(way, 0))(lambda way=way: table_copy(way, 0).start())
    for i in range(4):
        copies[i].wait()

    found = [
        find_slots(v_rcv_row[...], v_rcv_home[...], rcv_terms),
        find_slots(v_cmp_row[...], v_cmp_home[...], cmp_terms),
    ]
    lane = iota((count, 128), 1)
    req_rows = 2 * Z * plane
    req_iota = iota((req_rows, count), 0)
    wanted = ((req_iota >> 1) & (Z - 1)) * plane + req_iota // (2 * Z)
    slots, slot_rows, owner_rows, rank_hots = [], [], [], []
    request = jnp.zeros((req_rows, 128), F32)
    for kind, (owner, rank, place) in enumerate(found):
        owner_row = as_row(owner)
        slot = owner * pair + (kind * slot_cap + rank)
        rank_hot = lane == rank
        lhs = pick_mask((wanted == owner_row) & ((req_iota & 1) == kind))
        request = request + mm(lhs, jnp.where(rank_hot, place, 0.0).astype(BF))
        slots.append(slot)
        slot_rows.append(as_row(slot))
        owner_rows.append(owner_row)
        rank_hots.append(rank_hot)
    req_send[...] = request.reshape(plane, 2 * Z, 128)
    req_copies = [
        remote(
            req_send.at[peer(offset)], req_recv.at[p], req_ss.at[offset], req_rs.at[p],
            z * plane + peer(offset),
        )
        for offset in range(1, plane)
    ]
    for copy in req_copies:
        copy.start()
    req_recv[pl.ds(p, 1)] = req_send[pl.ds(p, 1)]

    for i in range(6, 14):
        copies[i].wait()

    def spectra(start, stop):
        @pl.loop(start, stop)
        def _(turn):
            here = pl.ds(pl.multiple_of(turn * ROWS, ROWS), ROWS)
            q[here, :], cross[here, :], last[here, :], power[here, :] = spectra_rows(
                v_traces[here, :], v_targets[here, :], v_twice[...], v_even[...], spec_x, spec_t
            )

    turns = count // ROWS
    spectra(0, turns // 4)

    for offset in range(1, plane):
        source = peer(offset)
        remote(
            req_send.at[source], req_recv.at[source], req_ss.at[offset], req_rs.at[source], me
        ).wait_recv()

    cap_bits = slot_cap.bit_length() - 1

    def value_copy(chunk, offset):
        return remote(
            vals.at[chunk, peer(offset)], fetched.at[chunk, p], val_ss.at[chunk, offset],
            val_rs.at[chunk, p], z * plane + peer(offset),
        )

    def serve(chunk):
        request_rows = req_recv[...].reshape(plane * 2 * Z, 128).astype(BF)
        row = iota((width, plane * 2 * Z), 0)
        col = iota((width, plane * 2 * Z), 1)
        kind = (row >> cap_bits) & 1
        expand = pick_mask(col == (row >> (cap_bits + 1)) * (2 * Z) + 2 * chunk + kind)
        wide = mm(expand, request_rows)
        row = iota((width, 128), 0)
        mine = (row & (slot_cap - 1)) == iota((width, 128), 1)
        place = mm(jnp.where(mine, wide, 0.0).astype(BF), jnp.ones((128, 128), BF)).astype(jnp.int32)
        place = place + ((row >> cap_bits) & 1) * rcv_terms
        onehot = jnp.concatenate(
            [pick_mask(iota((width, 128), 1) + base == place) for base in range(0, rows_all, 128)], axis=1
        )
        hot[chunk] = onehot
        vals[chunk] = exact_mm(onehot, table[chunk]).reshape(plane, pair, 128)
        for offset in range(1, plane):
            value_copy(chunk, offset).start()
        fetched[chunk, pl.ds(p, 1)] = vals[chunk, pl.ds(p, 1)]

    serve(z)
    marks = [turns // 4, turns // 2, 3 * turns // 4, turns]
    for distance in range(1, Z):
        for way in range(2):
            pl.when(arrives(way, distance))(lambda way=way: table_wait(way, distance))
            if distance < Z - 1:
                pl.when(goes_on(way, distance))(lambda way=way: table_copy(way, distance).start())
        for way in range(2):
            chunk = z - distance if way == 0 else z + distance
            pl.when(arrives(way, distance))(lambda chunk=chunk: serve(chunk))
        spectra(marks[distance - 1], marks[distance])

    mixed = src_rows(v_src_row[...], v_src_f[...])
    for chunk in range(Z):
        for offset in range(1, plane):
            source = peer(offset)
            remote(
                vals.at[chunk, source], fetched.at[chunk, source], val_ss.at[chunk, offset],
                val_rs.at[chunk, source], me,
            ).wait_recv()
        mixed = mixed + exact_mm(
            both_hot(slots, chunk * width, width), fetched[chunk].reshape(width, 128)
        )
    grads = gradients(
        mixed.astype(BF), q[...], cross[...], last[...], v_twice[...], v_tail[...], v_inverse[...]
    )
    live = iota((count, 128), 0) < counts[0]
    grads = jnp.where(live, grads, 0.0)
    powers = jnp.where(live, power[...], 0.0)
    grad_parts = split3(grads)
    power_parts = [split3(jnp.where(rank_hot, powers, 0.0)) for rank_hot in rank_hots]

    order = (3 * (1 - z // 2), (2 + 3 * z) % 5, 1 + z % 2, z)

    def grad_copy(chunk, offset):
        return remote(
            grad_send.at[chunk, peer(offset)], grad_recv.at[chunk, p], grad_ss.at[chunk, offset],
            grad_rs.at[chunk, p], z * plane + peer(offset),
        )

    for chunk in order:
        row = iota((width, count), 0) + chunk * width
        onehot = pick_mask((row == slot_rows[0]) | (row == slot_rows[1]))
        sent = mm(onehot, grad_parts[0]) + mm(onehot, grad_parts[1]) + mm(onehot, grad_parts[2])
        grad_send[chunk, :, pl.ds(0, pair), :] = sent.reshape(plane, pair, 128)
        row = iota((plane * 8, count), 0)
        energy = jnp.zeros((plane * 8, 128), F32)
        for kind in range(2):
            onehot = pick_mask(((row >> 3) + chunk * plane == owner_rows[kind]) & ((row & 7) == kind))
            for piece in power_parts[kind]:
                energy = energy + mm(onehot, piece)
        grad_send[chunk, :, pl.ds(pair, 8), :] = energy.reshape(plane, 8, 128)
        for offset in range(1, plane):
            grad_copy(chunk, offset).start()
        grad_recv[chunk, pl.ds(p, 1)] = grad_send[chunk, pl.ds(p, 1)]
    src_out[...] = settled_src(v_src_f[...], v_src_row[...], grads, powers)

    def part_copy(chunk, way):
        target = me + plane if way == 0 else me - plane
        return remote(
            part.at[chunk], inbox.at[way, chunk], part_ss.at[chunk], part_rs.at[way, chunk], target
        )

    def add_inbox(chunk, way):
        remote(
            part.at[chunk], inbox.at[way, chunk], part_ss.at[chunk], part_rs.at[way, chunk], me
        ).wait_recv()
        part[chunk] = part[chunk] + inbox[way, chunk]

    for step, chunk in enumerate(order):
        for offset in range(1, plane):
            source = peer(offset)
            remote(
                grad_send.at[chunk, source], grad_recv.at[chunk, source], grad_ss.at[chunk, offset],
                grad_rs.at[chunk, source], me,
            ).wait_recv()
        onehot = hot[chunk]
        got = split3(grad_recv[chunk, :, pl.ds(0, pair), :].reshape(width, 128))
        part[chunk, pl.ds(0, rows_all)] = mm_t(onehot, got[0]) + mm_t(onehot, got[1]) + mm_t(onehot, got[2])
        energy = grad_recv[chunk, :, pl.ds(pair, 8), :].reshape(plane * 8, 128)
        row, col = iota((plane * 8, width), 0), iota((plane * 8, width), 1)
        spread = pick_mask(
            ((row >> 3) == (col >> (cap_bits + 1))) & ((row & 7) == ((col >> cap_bits) & 1))
        )
        wide = sum(mm_t(piece, spread) for piece in split3(energy))
        mine = (iota((128, width), 1) & (slot_cap - 1)) == iota((128, width), 0)
        energy = jnp.sum(jnp.where(mine, wide, 0.0), axis=0, keepdims=True)
        energy = sum(mm(piece, onehot) for piece in split3(jnp.broadcast_to(energy, (8, width))))
        lines8 = iota((8, 128), 0)
        packed = jnp.zeros((8, 128), F32)
        for i in range(rows_all // 128):
            packed = packed + jnp.where(lines8 == i, energy[:, i * 128 : (i + 1) * 128], 0.0)
        part[chunk, pl.ds(rows_all, 8)] = packed
        pl.when((chunk >= z) & (z > 0))(lambda chunk=chunk: add_inbox(chunk, 0))
        pl.when((chunk <= z) & (z < Z - 1))(lambda chunk=chunk: add_inbox(chunk, 1))
        if step < Z - 1:
            pl.when(chunk > z)(lambda chunk=chunk: part_copy(chunk, 0).start())
            pl.when(chunk < z)(lambda chunk=chunk: part_copy(chunk, 1).start())

    packed = part[z, pl.ds(rows_all, 8)]
    for i in range(rows_all // 128):
        energy = jnp.transpose(jnp.broadcast_to(packed[i : i + 1, :], (128, 128)))
        here = pl.ds(i * 128, 128)
        updated = table[z, here] - STEP * part[z, here] / jnp.maximum(energy, 1.0)
        if i * 128 < rcv_terms:
            rcv_out[here, :] = updated
        else:
            cmp_out[pl.ds(i * 128 - rcv_terms, 128), :] = updated

    for copy in req_copies:
        copy.wait_send()
    for distance in range(Z - 1):
        for way in range(2):
            pl.when(goes_on(way, distance))(lambda way=way: table_copy(way, distance).wait_send())
    for chunk in range(Z):
        for offset in range(1, plane):
            value_copy(chunk, offset).wait_send()
            grad_copy(chunk, offset).wait_send()
        pl.when(z != chunk)(lambda chunk=chunk: part_copy(chunk, 0).wait_send())


def body(
    traces, targets, src_local, rcv_term, cmp_term, rcv_home, cmp_home, counts,
    src_filters, rcv_filters, cmp_filters,
):
    trace_rows, samples = traces.shape
    taps = src_filters.shape[1]
    device_count = lax.axis_size(AXES)
    lines = lax.axis_size("line")
    slot_cap = max(2, 2 * trace_rows // device_count)
    plane = device_count // Z
    pair = 2 * slot_cap
    blocks = samples // taps
    terms = (rcv_filters.shape[0], cmp_filters.shape[0])
    rows_all = sum(terms)
    tables = tuple(jnp.asarray(table) for table in spectral_tables(taps))
    shape = jax.ShapeDtypeStruct
    vmem, sem = pltpu.VMEM, pltpu.SemaphoreType.DMA
    operands = (
        traces, targets, src_local.reshape(1, -1), rcv_term.reshape(1, -1), cmp_term.reshape(1, -1),
        rcv_home.reshape(-1, 128), cmp_home.reshape(-1, 128),
        src_filters, rcv_filters, cmp_filters, *tables,
    )
    held = [vmem(x.shape, x.dtype) for x in operands[:8] + tables]
    return pl.pallas_call(
        functools.partial(fused_kernel, (lines, plane, slot_cap, terms)),
        out_shape=tuple(shape(x.shape, F32) for x in (src_filters, rcv_filters, cmp_filters)),
        in_specs=[pl.BlockSpec(memory_space=pltpu.SMEM)]
        + [pl.BlockSpec(memory_space=pl.ANY)] * len(operands),
        out_specs=(pl.BlockSpec(memory_space=pltpu.VMEM),) * 3,
        scratch_shapes=held
        + [
            vmem((Z, rows_all, 128), F32),
            vmem((plane, 2 * Z, 128), F32),
            vmem((plane, 2 * Z, 128), F32),
            vmem((Z, plane, pair, 128), F32),
            vmem((Z, plane, pair, 128), F32),
            vmem((Z, plane * pair, rows_all), BF),
            vmem((Z, plane, pair + 8, 128), F32),
            vmem((Z, plane, pair + 8, 128), F32),
            vmem((Z, rows_all + 8, 128), F32),
            vmem((2, Z, rows_all + 8, 128), F32),
            vmem((trace_rows, taps), F32),
            vmem((trace_rows, 2 * taps), F32),
            vmem((trace_rows, 2 * taps), F32),
            vmem((trace_rows, 128), F32),
            vmem((ROWS * blocks, 2 * taps), F32),
            vmem((ROWS * blocks, 2 * taps), F32),
            sem((14,)),
            sem((plane,)), sem((plane,)),
            sem((2, Z)), sem((2, Z + 1)),
            sem((Z, plane)), sem((Z, plane)),
            sem((Z, plane)), sem((Z, plane)),
            sem((Z,)), sem((2, Z)),
        ],
        compiler_params=pltpu.CompilerParams(
            vmem_limit_bytes=VMEM_LIMIT, collective_id=0, has_side_effects=True
        ),
        cost_estimate=pl.CostEstimate(
            flops=16 * trace_rows * samples * taps, bytes_accessed=6 * 2**20, transcendentals=0
        ),
    )(counts, *operands)


def solution(mesh):
    rows, flat = P(AXES, None), P(AXES)
    return jax.shard_map(
        body,
        mesh=mesh,
        in_specs=(rows, rows, flat, flat, flat, P(), P(), flat, rows, rows, rows),
        out_specs=(rows, rows, rows),
        check_vma=False,
    )
```

time: 104 us -> 79.4 us (0.76)
  waiting for transfers between devices: 47.4 us -> 0 us
  Pallas kernels: 17.5 us -> 62.8 us
  blocking collectives: 14.4 us -> 0 us
  starting transfers between devices: 9.56 us -> 0 us
  local copies, waits for them, and re-layouts: 12.8 us -> 14.7 us
    all_to_all x3 -> x0, waiting for transfers between devices: 47.4 us -> none  [exchange(): return lax.all_to_all(value, AXES, split_axis=1, concat_axis=1, tiled=True)]
    pallas_call x5 -> x1, Pallas kernels: 17.5 us -> 62.8 us  [body(): pl.pallas_call(functools.partial(fused_kernel, (lines, plane, slot_cap, t...]
    all_to_all x1 -> x0, blocking collectives: 14.4 us -> none  [exchange(): return lax.all_to_all(value, AXES, split_axis=1, concat_axis=1, tiled=True)]
    all_to_all x3 -> x0, starting transfers between devices: 9.56 us -> none  [exchange(): return lax.all_to_all(value, AXES, split_axis=1, concat_axis=1, tiled=True)]
    unnamed x38 -> x31, local copies, waits for them, and re-layouts: 8.49 us -> 14.7 us
    reshape x2 -> x0, local copies, waits for them, and re-layouts: 2.16 us -> none  [the longest x1 1.11 us: body(): send.reshape(2, device_count, slot_cap, taps)]
    all_to_all x4 -> x0, local copies, waits for them, and re-layouts: 1.43 us -> none  [exchange(): return lax.all_to_all(value, AXES, split_axis=1, concat_axis=1, tiled=True)]
  transfers between devices with their start and end apart: 3 -> 0, of which waited for: 3 -> 0; matrix products, arithmetic and copies ran while one was open for 1% -> 0% of each run, Pallas kernels for 6% -> 0%
where the time goes in v2:
time: 79.4 us; the launch traced here: 78.8 us
  Pallas kernels  62.8 us (79%)
  local copies, waits for them, and re-layouts  14.7 us (19%)
  between operations  1.31 us (2%)
    pallas_call x1, Pallas kernels, body(): pl.pallas_call(functools.partial(fused_kernel, (lines, plane, slot_cap, t...  62.8 us
    unnamed x31, local copies, waits for them, and re-layouts  14.7 us

profile of v2, /device:TPU:0, one launch (start us, length us, event | category | flops | bytes accessed | tf_op | source)
XLA Modules:
  0.0 78.8 jit_solution(1596874173169224534)
XLA Ops:
  1.3 0.0 copy-start
  1.3 1.6 %copy-done = bf16[512,2048]{1,0:T(8,128)(2,1)S(1)} copy-done((bf16[512,2048]{1,0:T(8,128)(2,1)S(1)}, bf16[512,2048]{1,0:T(8,128)(2,1)}, u32[]{:S(2)}) %copy-start) | copy-done | bytes 2097176
  2.9 0.0 copy-start.1
  2.9 1.6 %copy-done.1 = bf16[512,2048]{1,0:T(8,128)(2,1)S(1)} copy-done((bf16[512,2048]{1,0:T(8,128)(2,1)S(1)}, bf16[512,2048]{1,0:T(8,128)(2,1)}, u32[]{:S(2)}) %copy-start.1) | copy-done | bytes 2097176
  4.5 0.0 copy-start.2
  4.5 0.9 %copy-done.2 = f32[256,128]{1,0:T(8,128)S(1)} copy-done((f32[256,128]{1,0:T(8,128)S(1)}, f32[256,128]{1,0:T(8,128)}, u32[]{:S(2)}) %copy-start.2) | copy-done | bytes 131096
  5.4 0.0 copy-start.3
  5.4 0.8 %copy-done.3 = f32[128,128]{1,0:T(8,128)S(1)} copy-done((f32[128,128]{1,0:T(8,128)S(1)}, f32[128,128]{1,0:T(8,128)}, u32[]{:S(2)}) %copy-start.3) | copy-done | bytes 65560
  6.2 0.0 copy-start.4
  6.2 0.8 copy-done.4
  7.0 0.0 copy-start.5
  7.0 0.7 copy-done.5
  7.7 0.7 copy-done.6
  8.4 0.7 copy-done.7
  9.1 0.7 copy-done.8
  9.7 0.7 copy-done.9
  10.4 1.0 %copy-done.10 = bf16[768,256]{1,0:T(8,128)(2,1)S(1)} copy-done((bf16[768,256]{1,0:T(8,128)(2,1)S(1)}, bf16[768,256]{1,0:T(8,128)(2,1)}, u32[]{:S(2)}) %copy-start.10) | copy-done | bytes 393240
  11.4 0.9 %copy-done.11 = bf16[768,128]{1,0:T(8,128)(2,1)S(1)} copy-done((bf16[768,128]{1,0:T(8,128)(2,1)S(1)}, bf16[768,128]{1,0:T(8,128)(2,1)}, u32[]{:S(2)}) %copy-start.11) | copy-done | bytes 196632
  12.3 0.9 %copy-done.12 = bf16[768,128]{1,0:T(8,128)(2,1)S(1)} copy-done((bf16[768,128]{1,0:T(8,128)(2,1)S(1)}, bf16[768,128]{1,0:T(8,128)(2,1)}, u32[]{:S(2)}) %copy-start.12) | copy-done | bytes 196632
  13.3 0.9 %copy-done.13 = bf16[256,256]{1,0:T(8,128)(2,1)S(1)} copy-done((bf16[256,256]{1,0:T(8,128)(2,1)S(1)}, bf16[256,256]{1,0:T(8,128)(2,1)}, u32[]{:S(2)}) %copy-start.13) | copy-done | bytes 131096
  14.2 62.8 %shard_map.166 = (f32[4,128]{1,0:T(4,128)S(1)}, f32[128,128]{1,0:T(8,128)S(1)}, f32[256,128]{1,0:T(8,128)S(1)}) custom-call(s32[1]{0:T(128)S(6)} %copy.21.counts, bf16[512,2048]{1,0:T(8,128)(2,1)S(1)} %copy-done, bf16[512,2048]{1,0:T(8,128)(2,1)S(1)} %copy-done.1, s32[1,512]{1,0:T(1,128)S(1)} %bitcast.7, s32[1,512]{1,0:T(1,128)S(1)} %bitcast.8, ...), custom_call_target="tpu_custom_call" | custom-call | flops 2147483648 | bytes 6291456 | tf_op jit(solution)/shard_map/pallas_call | solution.py:502
  77.0 0.6 copy.22
  77.5 0.6 copy.23
  78.2 0.7 copy.24
  (8 shorter events, 0.0 us)
Async XLA Ops:
  1.3 1.6 %copy-start = (bf16[512,2048]{1,0:T(8,128)(2,1)S(1)}, bf16[512,2048]{1,0:T(8,128)(2,1)}, u32[]{:S(2)}) copy-start(bf16[512,2048]{1,0:T(8,128)(2,1)} %traces.1) | copy-start | bytes 6291460
  2.9 1.6 %copy-start.1 = (bf16[512,2048]{1,0:T(8,128)(2,1)S(1)}, bf16[512,2048]{1,0:T(8,128)(2,1)}, u32[]{:S(2)}) copy-start(bf16[512,2048]{1,0:T(8,128)(2,1)} %targets.1) | copy-start | bytes 6291460
  4.5 0.9 %copy-start.2 = (f32[256,128]{1,0:T(8,128)S(1)}, f32[256,128]{1,0:T(8,128)}, u32[]{:S(2)}) copy-start(f32[256,128]{1,0:T(8,128)} %cmp_f.1) | copy-start | bytes 393220
  5.4 0.8 %copy-start.3 = (f32[128,128]{1,0:T(8,128)S(1)}, f32[128,128]{1,0:T(8,128)}, u32[]{:S(2)}) copy-start(f32[128,128]{1,0:T(8,128)} %rcv_f.1) | copy-start | bytes 196612
  6.2 0.8 copy-start.4
  7.0 0.7 copy-start.5
  7.7 0.7 copy-start.6
  8.4 0.7 copy-start.7
  9.0 0.7 copy-start.8
  9.7 0.7 copy-start.9
  10.4 1.0 %copy-start.10 = (bf16[768,256]{1,0:T(8,128)(2,1)S(1)}, bf16[768,256]{1,0:T(8,128)(2,1)}, u32[]{:S(2)}) copy-start(bf16[768,256]{1,0:T(8,128)(2,1)} %constant.10.clone.tail) | copy-start | bytes 1179652
  11.4 0.9 %copy-start.11 = (bf16[768,128]{1,0:T(8,128)(2,1)S(1)}, bf16[768,128]{1,0:T(8,128)(2,1)}, u32[]{:S(2)}) copy-start(bf16[768,128]{1,0:T(8,128)(2,1)} %constant.11.clone.inverse) | copy-start | bytes 589828
  12.3 0.9 %copy-start.12 = (bf16[768,128]{1,0:T(8,128)(2,1)S(1)}, bf16[768,128]{1,0:T(8,128)(2,1)}, u32[]{:S(2)}) copy-start(bf16[768,128]{1,0:T(8,128)(2,1)} %constant.9.clone.even) | copy-start | bytes 589828
  13.3 0.9 %copy-start.13 = (bf16[256,256]{1,0:T(8,128)(2,1)S(1)}, bf16[256,256]{1,0:T(8,128)(2,1)}, u32[]{:S(2)}) copy-start(bf16[256,256]{1,0:T(8,128)(2,1)} %constant.8.clone.twice) | copy-start | bytes 393220

commit v3 on v2

--- a/solution.py
+++ b/solution.py
@@ -14,7 +14,7 @@
 AXES = ("shot", "line")
 ROWS = 64
 Z = 4
-VMEM_LIMIT = 48 * 1024 * 1024
+VMEM_LIMIT = 60 * 1024 * 1024
 
 
 def halves(matrix):
@@ -38,10 +38,13 @@
         high, low = halves(matrix)
         return np.concatenate([high, high, low], axis=0)
 
+    def tall(matrix):
+        return np.concatenate([matrix[:, :128], matrix[:, 128:]], axis=0)
+
     return (
-        twice,
+        tall(twice),
         triple(inverse[:, :taps] @ even),
-        triple(inverse[:, taps:] @ forward[taps:]),
+        tall(triple(inverse[:, taps:] @ forward[taps:])),
         triple(inverse[:, :taps]),
     )
 
@@ -54,17 +57,18 @@
     return lax.dot_general(left, right, (((0,), (0,)), ((), ())), preferred_element_type=F32)
 
 
-def split3(value):
+def split2(value):
     high = value.astype(BF)
-    rest = value - high.astype(F32)
-    middle = rest.astype(BF)
-    low = (rest - middle.astype(F32)).astype(BF)
-    return high, middle, low
-
-
-def exact_mm(onehot, value):
-    high, middle, low = split3(value)
-    return mm(onehot, high) + mm(onehot, middle) + mm(onehot, low)
+    return jnp.concatenate([high, (value - high.astype(F32)).astype(BF)], axis=1)
+
+
+def folded(wide):
+    half = wide.shape[1] // 2
+    return wide[:, :half] + wide[:, half:]
+
+
+def pick_mm(onehot, parts):
+    return folded(mm(onehot, parts))
 
 
 def fine_mm(value, table):
@@ -180,20 +184,15 @@
     return fine_mm(jnp.concatenate([gr, gi], axis=1), inverse)
 
 
-def settled_src(filters, src_row, grads, power):
+def settled_src(filters, here, grads, energy):
     terms = filters.shape[0]
-    here = pick_mask(iota((8, src_row.shape[1]), 0) == src_row)
-    sums = exact_mm(here, grads)[:terms]
-    energy = exact_mm(here, power)[:terms]
-    return filters - STEP * sums / jnp.maximum(energy, 1.0)
-
-
-def src_rows(src_row, src_filters):
-    here = pick_mask(iota((8, src_row.shape[1]), 0) == src_row)
-    high, middle, low = split3(
-        jnp.concatenate([src_filters, jnp.zeros((8 - src_filters.shape[0], src_filters.shape[1]), F32)], axis=0)
-    )
-    return mm_t(here, high) + mm_t(here, middle) + mm_t(here, low)
+    sums = pick_mm(here, split2(grads))[:terms]
+    return filters - STEP * sums / jnp.maximum(energy[:terms], 1.0)
+
+
+def src_rows(here, src_filters):
+    missing = jnp.zeros((8 - src_filters.shape[0], src_filters.shape[1]), F32)
+    return folded(mm_t(here, split2(jnp.concatenate([src_filters, missing], axis=0))))
 
 
 def fused_kernel(
@@ -203,7 +202,7 @@
     v_traces, v_targets, v_src_row, v_rcv_row, v_cmp_row, v_rcv_home, v_cmp_home,
     v_src_f, v_twice, v_even, v_tail, v_inverse,
     table, req_send, req_recv, vals, fetched, hot, grad_send, grad_recv, part, inbox,
-    q, cross, last, power, spec_x, spec_t,
+    mixed, slot_hot, slot_hot_t, q, cross, last, power, spec_x, spec_t,
     local_sem, req_ss, req_rs, tab_ss, tab_rs, val_ss, val_rs, grad_ss, grad_rs, part_ss, part_rs,
 ):
     lines, plane, slot_cap, terms = sizes
@@ -230,9 +229,12 @@
     small = [
         (rcv_row, v_rcv_row), (cmp_row, v_cmp_row), (rcv_home, v_rcv_home), (cmp_home, v_cmp_home),
         (rcv_f, table.at[z, pl.ds(0, rcv_terms)]), (cmp_f, table.at[z, pl.ds(rcv_terms, cmp_terms)]),
-        (src_row, v_src_row), (src_f, v_src_f), (twice, v_twice), (even, v_even),
-        (tail, v_tail), (inverse, v_inverse), (traces, v_traces), (targets, v_targets),
+        (src_row, v_src_row), (src_f, v_src_f), (even, v_even), (inverse, v_inverse),
+        (traces, v_traces), (targets, v_targets),
     ]
+    for source, target in ((twice, v_twice), (tail, v_tail)):
+        high = target.shape[0]
+        small += [(source.at[pl.ds(i * high, high)], target.at[:, pl.ds(i * 128, 128)]) for i in range(2)]
     copies = [
         pltpu.make_async_copy(source, target, local_sem.at[i]) for i, (source, target) in enumerate(small)
     ]
@@ -307,7 +309,7 @@
         copy.start()
     req_recv[pl.ds(p, 1)] = req_send[pl.ds(p, 1)]
 
-    for i in range(6, 14):
+    for i in range(6, 16):
         copies[i].wait()
 
     def spectra(start, stop):
@@ -349,43 +351,64 @@
         onehot = jnp.concatenate(
             [pick_mask(iota((width, 128), 1) + base == place) for base in range(0, rows_all, 128)], axis=1
         )
-        hot[chunk] = onehot
-        vals[chunk] = exact_mm(onehot, table[chunk]).reshape(plane, pair, 128)
+        vals[chunk] = pick_mm(onehot, split2(table[chunk])).reshape(plane, pair, 128)
         for offset in range(1, plane):
             value_copy(chunk, offset).start()
         fetched[chunk, pl.ds(p, 1)] = vals[chunk, pl.ds(p, 1)]
-
-    serve(z)
-    marks = [turns // 4, turns // 2, 3 * turns // 4, turns]
-    for distance in range(1, Z):
-        for way in range(2):
-            pl.when(arrives(way, distance))(lambda way=way: table_wait(way, distance))
-            if distance < Z - 1:
-                pl.when(goes_on(way, distance))(lambda way=way: table_copy(way, distance).start())
-        for way in range(2):
-            chunk = z - distance if way == 0 else z + distance
-            pl.when(arrives(way, distance))(lambda chunk=chunk: serve(chunk))
-        spectra(marks[distance - 1], marks[distance])
-
-    mixed = src_rows(v_src_row[...], v_src_f[...])
-    for chunk in range(Z):
+        hot[chunk] = pick_mask(iota((rows_all, width), 0) == as_row(place))
+
+    def take(chunk):
         for offset in range(1, plane):
             source = peer(offset)
             remote(
                 vals.at[chunk, source], fetched.at[chunk, source], val_ss.at[chunk, offset],
                 val_rs.at[chunk, source], me,
             ).wait_recv()
-        mixed = mixed + exact_mm(
-            both_hot(slots, chunk * width, width), fetched[chunk].reshape(width, 128)
-        )
+        mixed[...] += pick_mm(slot_hot[chunk], split2(fetched[chunk].reshape(width, 128)))
+
+    serve(z)
+    src_hot = pick_mask(iota((8, count), 0) == v_src_row[...])
+    mixed[...] = src_rows(src_hot, v_src_f[...])
+
+    def near(act, distance):
+        if distance == 0:
+            act(z)
+            return
+        for way in range(2):
+            chunk = z - distance if way == 0 else z + distance
+            pl.when(arrives(way, distance))(lambda chunk=chunk: act(chunk))
+
+    marks = [turns // 4, 5 * turns // 8, turns, turns]
+    for distance in range(1, Z):
+        for way in range(2):
+            pl.when(arrives(way, distance))(lambda way=way: table_wait(way, distance))
+            if distance < Z - 1:
+                pl.when(goes_on(way, distance))(lambda way=way: table_copy(way, distance).start())
+        near(serve, distance)
+        if distance == 1:
+            for chunk in range(Z):
+                slot_hot[chunk] = both_hot(slots, chunk * width, width)
+        spectra(marks[distance - 1], marks[distance])
+        if distance == 2:
+            powers = jnp.where(iota((count, 128), 0) < counts[0], power[...], 0.0)
+            row = iota((Z * plane * 8, count), 0)
+            energy = jnp.zeros((Z * plane * 8, 128), F32)
+            for kind in range(2):
+                onehot = pick_mask(((row >> 3) == owner_rows[kind]) & ((row & 7) == kind))
+                energy = energy + pick_mm(onehot, split2(jnp.where(rank_hots[kind], powers, 0.0)))
+            grad_send[:, :, pl.ds(pair, 8), :] = energy.reshape(Z, plane, 8, 128)
+            src_energy = pick_mm(src_hot, split2(powers))
+            for chunk in range(Z):
+                row = iota((width, count), 0) + chunk * width
+                slot_hot_t[chunk] = pick_mask((row == slot_rows[0]) | (row == slot_rows[1]))
+        near(take, distance - 1)
+    near(take, Z - 1)
+
     grads = gradients(
-        mixed.astype(BF), q[...], cross[...], last[...], v_twice[...], v_tail[...], v_inverse[...]
+        mixed[...].astype(BF), q[...], cross[...], last[...], v_twice[...], v_tail[...], v_inverse[...]
     )
-    live = iota((count, 128), 0) < counts[0]
-    grads = jnp.where(live, grads, 0.0)
-    powers = jnp.where(live, power[...], 0.0)
-    grad_parts = split3(grads)
-    power_parts = [split3(jnp.where(rank_hot, powers, 0.0)) for rank_hot in rank_hots]
+    grads = jnp.where(iota((count, 128), 0) < counts[0], grads, 0.0)
+    grad_parts = split2(grads)
 
     order = (3 * (1 - z // 2), (2 + 3 * z) % 5, 1 + z % 2, z)
 
@@ -396,21 +419,12 @@
         )
 
     for chunk in order:
-        row = iota((width, count), 0) + chunk * width
-        onehot = pick_mask((row == slot_rows[0]) | (row == slot_rows[1]))
-        sent = mm(onehot, grad_parts[0]) + mm(onehot, grad_parts[1]) + mm(onehot, grad_parts[2])
+        sent = pick_mm(slot_hot_t[chunk], grad_parts)
         grad_send[chunk, :, pl.ds(0, pair), :] = sent.reshape(plane, pair, 128)
-        row = iota((plane * 8, count), 0)
-        energy = jnp.zeros((plane * 8, 128), F32)
-        for kind in range(2):
-            onehot = pick_mask(((row >> 3) + chunk * plane == owner_rows[kind]) & ((row & 7) == kind))
-            for piece in power_parts[kind]:
-                energy = energy + mm(onehot, piece)
-        grad_send[chunk, :, pl.ds(pair, 8), :] = energy.reshape(plane, 8, 128)
         for offset in range(1, plane):
             grad_copy(chunk, offset).start()
         grad_recv[chunk, pl.ds(p, 1)] = grad_send[chunk, pl.ds(p, 1)]
-    src_out[...] = settled_src(v_src_f[...], v_src_row[...], grads, powers)
+    src_out[...] = settled_src(v_src_f[...], src_hot, grads, src_energy)
 
     def part_copy(chunk, way):
         target = me + plane if way == 0 else me - plane
@@ -432,17 +446,20 @@
                 grad_rs.at[chunk, source], me,
             ).wait_recv()
         onehot = hot[chunk]
-        got = split3(grad_recv[chunk, :, pl.ds(0, pair), :].reshape(width, 128))
-        part[chunk, pl.ds(0, rows_all)] = mm_t(onehot, got[0]) + mm_t(onehot, got[1]) + mm_t(onehot, got[2])
+        got = split2(grad_recv[chunk, :, pl.ds(0, pair), :].reshape(width, 128))
+        part[chunk, pl.ds(0, rows_all)] = pick_mm(onehot, got)
         energy = grad_recv[chunk, :, pl.ds(pair, 8), :].reshape(plane * 8, 128)
         row, col = iota((plane * 8, width), 0), iota((plane * 8, width), 1)
         spread = pick_mask(
             ((row >> 3) == (col >> (cap_bits + 1))) & ((row & 7) == ((col >> cap_bits) & 1))
         )
-        wide = sum(mm_t(piece, spread) for piece in split3(energy))
-        mine = (iota((128, width), 1) & (slot_cap - 1)) == iota((128, width), 0)
+        wide = mm_t(split2(energy), spread)
+        mine = (iota((256, width), 1) & (slot_cap - 1)) == (iota((256, width), 0) & 127)
         energy = jnp.sum(jnp.where(mine, wide, 0.0), axis=0, keepdims=True)
-        energy = sum(mm(piece, onehot) for piece in split3(jnp.broadcast_to(energy, (8, width))))
+        high = energy.astype(BF).astype(F32)
+        energy = jnp.where(iota((8, width), 0) < 4, high, energy - high).astype(BF)
+        energy = lax.dot_general(energy, onehot, (((1,), (1,)), ((), ())), preferred_element_type=F32)
+        energy = energy[0:1] + energy[4:5]
         lines8 = iota((8, 128), 0)
         packed = jnp.zeros((8, 128), F32)
         for i in range(rows_all // 128):
@@ -498,12 +515,13 @@
         rcv_home.reshape(-1, 128), cmp_home.reshape(-1, 128),
         src_filters, rcv_filters, cmp_filters, *tables,
     )
-    held = [vmem(x.shape, x.dtype) for x in operands[:8] + tables]
+    held = [vmem(x.shape, x.dtype) for x in operands[:8]]
+    held += [vmem((x.shape[0] * 128 // w, w), x.dtype) for x, w in zip(tables, (256, 128, 256, 128))]
     return pl.pallas_call(
         functools.partial(fused_kernel, (lines, plane, slot_cap, terms)),
         out_shape=tuple(shape(x.shape, F32) for x in (src_filters, rcv_filters, cmp_filters)),
         in_specs=[pl.BlockSpec(memory_space=pltpu.SMEM)]
-        + [pl.BlockSpec(memory_space=pl.ANY)] * len(operands),
+        + [pl.BlockSpec(memory_space=pltpu.HBM)] * len(operands),
         out_specs=(pl.BlockSpec(memory_space=pltpu.VMEM),) * 3,
         scratch_shapes=held
         + [
@@ -512,18 +530,21 @@
             vmem((plane, 2 * Z, 128), F32),
             vmem((Z, plane, pair, 128), F32),
             vmem((Z, plane, pair, 128), F32),
-            vmem((Z, plane * pair, rows_all), BF),
+            vmem((Z, rows_all, plane * pair), BF),
             vmem((Z, plane, pair + 8, 128), F32),
             vmem((Z, plane, pair + 8, 128), F32),
             vmem((Z, rows_all + 8, 128), F32),
             vmem((2, Z, rows_all + 8, 128), F32),
+            vmem((trace_rows, taps), F32),
+            vmem((Z, trace_rows, plane * pair), BF),
+            vmem((Z, plane * pair, trace_rows), BF),
             vmem((trace_rows, taps), F32),
             vmem((trace_rows, 2 * taps), F32),
             vmem((trace_rows, 2 * taps), F32),
             vmem((trace_rows, 128), F32),
             vmem((ROWS * blocks, 2 * taps), F32),
             vmem((ROWS * blocks, 2 * taps), F32),
-            sem((14,)),
+            sem((16,)),
             sem((plane,)), sem((plane,)),
             sem((2, Z)), sem((2, Z + 1)),
             sem((Z, plane)), sem((Z, plane)),

time: 79.4 us -> 63.3 us (0.80)
  local copies, waits for them, and re-layouts: 14.7 us -> 4.27 us
  Pallas kernels: 62.8 us -> 57.5 us
    unnamed x31 -> x3, local copies, waits for them, and re-layouts: 14.7 us -> 4.27 us
    pallas_call x1, Pallas kernels: 62.8 us -> 57.5 us  [body(): pl.pallas_call(functools.partial(fused_kernel, (lines, plane, slot_cap, t...]
where the time goes in v3:
time: 63.3 us; the launch traced here: 63.1 us
  Pallas kernels  57.5 us (91%)
  local copies, waits for them, and re-layouts  4.27 us (7%)
  between operations  1.29 us (2%)
    pallas_call x1, Pallas kernels, body(): pl.pallas_call(functools.partial(fused_kernel, (lines, plane, slot_cap, t...  57.5 us
    unnamed x3, local copies, waits for them, and re-layouts  4.27 us

profile of v3, /device:TPU:0, one launch (start us, length us, event | category | flops | bytes accessed | tf_op | source)
XLA Modules:
  0.0 63.1 jit_solution(763517895569240084)
XLA Ops:
  1.3 57.5 %shard_map.166 = (f32[4,128]{1,0:T(4,128)}, f32[128,128]{1,0:T(8,128)}, f32[256,128]{1,0:T(8,128)}) custom-call(s32[1]{0:T(128)S(6)} %copy.21.counts, bf16[512,2048]{1,0:T(8,128)(2,1)} %traces.1, bf16[512,2048]{1,0:T(8,128)(2,1)} %targets.1, s32[1,512]{1,0:T(1,128)} %bitcast.7, s32[1,512]{1,0:T(1,128)} %bitcast.8, s32[1,512]{1,0:T(1,128)} %bitcast.9, ...), custom_call_target="tpu_custom_call" | custom-call | flops 2147483648 | bytes 6291456 | tf_op jit(solution)/shard_map/pallas_call | solution.py:520
  58.8 1.2 %copy.22 = f32[4,128]{1,0:T(4,128)} copy(f32[4,128]{1,0:T(4,128)} %get-tuple-element.6) | data formatting | bytes 4096
  60.0 1.5 %copy.23 = f32[128,128]{1,0:T(8,128)} copy(f32[128,128]{1,0:T(8,128)} %get-tuple-element.7) | data formatting | bytes 131072
  61.5 1.6 %copy.24 = f32[256,128]{1,0:T(8,128)} copy(f32[256,128]{1,0:T(8,128)} %get-tuple-element.8) | data formatting | bytes 262144

commit v4 on v3

--- a/solution.py
+++ b/solution.py
@@ -185,9 +185,9 @@
 
 
 def settled_src(filters, here, grads, energy):
-    terms = filters.shape[0]
-    sums = pick_mm(here, split2(grads))[:terms]
-    return filters - STEP * sums / jnp.maximum(energy[:terms], 1.0)
+    missing = jnp.zeros((8 - filters.shape[0], filters.shape[1]), F32)
+    sums = pick_mm(here, split2(grads))
+    return jnp.concatenate([filters, missing], axis=0) - STEP * sums / jnp.maximum(energy, 1.0)
 
 
 def src_rows(here, src_filters):
@@ -198,7 +198,7 @@
 def fused_kernel(
     sizes, counts, traces, targets, src_row, rcv_row, cmp_row, rcv_home, cmp_home,
     src_f, rcv_f, cmp_f, twice, even, tail, inverse,
-    src_out, rcv_out, cmp_out,
+    out,
     v_traces, v_targets, v_src_row, v_rcv_row, v_cmp_row, v_rcv_home, v_cmp_home,
     v_src_f, v_twice, v_even, v_tail, v_inverse,
     table, req_send, req_recv, vals, fetched, hot, grad_send, grad_recv, part, inbox,
@@ -226,6 +226,16 @@
             device_id=device(index), device_id_type=pl.DeviceIdType.MESH,
         )
 
+    barrier = pltpu.get_barrier_semaphore()
+
+    def greet(index):
+        pl.semaphore_signal(barrier, inc=1, device_id=device(index), device_id_type=pl.DeviceIdType.MESH)
+
+    for distance in range(1, Z):
+        greet((z + distance) % Z * plane + p)
+    for offset in range(1, plane):
+        greet(z * plane + peer(offset))
+
     small = [
         (rcv_row, v_rcv_row), (cmp_row, v_cmp_row), (rcv_home, v_rcv_home), (cmp_home, v_cmp_home),
         (rcv_f, table.at[z, pl.ds(0, rcv_terms)]), (cmp_f, table.at[z, pl.ds(rcv_terms, cmp_terms)]),
@@ -240,28 +250,23 @@
     ]
     for copy in copies:
         copy.start()
-    barrier = pltpu.get_barrier_semaphore()
-
-    def greet(index):
-        pl.semaphore_signal(barrier, inc=1, device_id=device(index), device_id_type=pl.DeviceIdType.MESH)
-
-    for offset in range(1, plane):
-        greet(z * plane + peer(offset))
-    for distance in range(1, Z):
-        greet((z + distance) % Z * plane + p)
     pl.semaphore_wait(barrier, plane - 1 + Z - 1)
 
-    def table_copy(way, distance):
+    half = rows_all // 2
+
+    def table_copy(way, distance, piece):
         chunk = z - distance if way == 0 else z + distance
         target = me + plane if way == 0 else me - plane
+        rows = table.at[chunk, pl.ds(piece * half, half)]
         return remote(
-            table.at[chunk], table.at[chunk], tab_ss.at[way, distance], tab_rs.at[way, distance + 1], target
-        )
-
-    def table_wait(way, distance):
+            rows, rows, tab_ss.at[way, distance, piece], tab_rs.at[way, distance + 1, piece], target
+        )
+
+    def table_wait(way, distance, piece):
         chunk = z - distance if way == 0 else z + distance
+        rows = table.at[chunk, pl.ds(piece * half, half)]
         remote(
-            table.at[chunk], table.at[chunk], tab_ss.at[way, distance], tab_rs.at[way, distance], me
+            rows, rows, tab_ss.at[way, distance, piece], tab_rs.at[way, distance, piece], me
         ).wait_recv()
 
     def arrives(way, distance):
@@ -272,8 +277,9 @@
 
     copies[4].wait()
     copies[5].wait()
-    for way in range(2):
-        pl.when(goes_on(way, 0))(lambda way=way: table_copy(way, 0).start())
+    for piece in range(2):
+        for way in range(2):
+            pl.when(goes_on(way, 0))(lambda way=way, piece=piece: table_copy(way, 0, piece).start())
     for i in range(4):
         copies[i].wait()
 
@@ -380,10 +386,13 @@
 
     marks = [turns // 4, 5 * turns // 8, turns, turns]
     for distance in range(1, Z):
-        for way in range(2):
-            pl.when(arrives(way, distance))(lambda way=way: table_wait(way, distance))
-            if distance < Z - 1:
-                pl.when(goes_on(way, distance))(lambda way=way: table_copy(way, distance).start())
+        for piece in range(2):
+            for way in range(2):
+                pl.when(arrives(way, distance))(lambda way=way, piece=piece: table_wait(way, distance, piece))
+                if distance < Z - 1:
+                    pl.when(goes_on(way, distance))(
+                        lambda way=way, piece=piece: table_copy(way, distance, piece).start()
+                    )
         near(serve, distance)
         if distance == 1:
             for chunk in range(Z):
@@ -424,19 +433,26 @@
         for offset in range(1, plane):
             grad_copy(chunk, offset).start()
         grad_recv[chunk, pl.ds(p, 1)] = grad_send[chunk, pl.ds(p, 1)]
-    src_out[...] = settled_src(v_src_f[...], src_hot, grads, src_energy)
-
-    def part_copy(chunk, way):
+    out[pl.ds(rows_all, 8)] = settled_src(v_src_f[...], src_hot, grads, src_energy)
+
+    cut = rows_all // 16 * 8
+    spans = (pl.ds(0, cut), pl.ds(cut, rows_all + 8 - cut))
+
+    def part_copy(chunk, way, piece):
         target = me + plane if way == 0 else me - plane
+        rows = spans[piece]
         return remote(
-            part.at[chunk], inbox.at[way, chunk], part_ss.at[chunk], part_rs.at[way, chunk], target
-        )
-
-    def add_inbox(chunk, way):
+            part.at[chunk, rows], inbox.at[way, chunk, rows], part_ss.at[chunk, piece],
+            part_rs.at[way, chunk, piece], target,
+        )
+
+    def add_inbox(chunk, way, piece):
+        rows = spans[piece]
         remote(
-            part.at[chunk], inbox.at[way, chunk], part_ss.at[chunk], part_rs.at[way, chunk], me
+            part.at[chunk, rows], inbox.at[way, chunk, rows], part_ss.at[chunk, piece],
+            part_rs.at[way, chunk, piece], me,
         ).wait_recv()
-        part[chunk] = part[chunk] + inbox[way, chunk]
+        part[chunk, rows] = part[chunk, rows] + inbox[way, chunk, rows]
 
     for step, chunk in enumerate(order):
         for offset in range(1, plane):
@@ -465,32 +481,53 @@
         for i in range(rows_all // 128):
             packed = packed + jnp.where(lines8 == i, energy[:, i * 128 : (i + 1) * 128], 0.0)
         part[chunk, pl.ds(rows_all, 8)] = packed
-        pl.when((chunk >= z) & (z > 0))(lambda chunk=chunk: add_inbox(chunk, 0))
-        pl.when((chunk <= z) & (z < Z - 1))(lambda chunk=chunk: add_inbox(chunk, 1))
-        if step < Z - 1:
-            pl.when(chunk > z)(lambda chunk=chunk: part_copy(chunk, 0).start())
-            pl.when(chunk < z)(lambda chunk=chunk: part_copy(chunk, 1).start())
+        for piece in range(2):
+            def pass_on(way, chunk=chunk, piece=piece):
+                pl.when(z > 0 if way == 0 else z < Z - 1)(lambda: add_inbox(chunk, way, piece))
+                if step < Z - 1:
+                    part_copy(chunk, way, piece).start()
+
+            pl.when(chunk >= z)(lambda: pass_on(0))
+            pl.when(chunk <= z)(lambda: pass_on(1))
 
     packed = part[z, pl.ds(rows_all, 8)]
     for i in range(rows_all // 128):
         energy = jnp.transpose(jnp.broadcast_to(packed[i : i + 1, :], (128, 128)))
         here = pl.ds(i * 128, 128)
         updated = table[z, here] - STEP * part[z, here] / jnp.maximum(energy, 1.0)
-        if i * 128 < rcv_terms:
-            rcv_out[here, :] = updated
-        else:
-            cmp_out[pl.ds(i * 128 - rcv_terms, 128), :] = updated
+        out[here, :] = updated
 
     for copy in req_copies:
         copy.wait_send()
     for distance in range(Z - 1):
         for way in range(2):
-            pl.when(goes_on(way, distance))(lambda way=way: table_copy(way, distance).wait_send())
+            for piece in range(2):
+                pl.when(goes_on(way, distance))(
+                    lambda way=way, piece=piece: table_copy(way, distance, piece).wait_send()
+                )
     for chunk in range(Z):
         for offset in range(1, plane):
             value_copy(chunk, offset).wait_send()
             grad_copy(chunk, offset).wait_send()
-        pl.when(z != chunk)(lambda chunk=chunk: part_copy(chunk, 0).wait_send())
+        for piece in range(2):
+            pl.when(z != chunk)(lambda chunk=chunk, piece=piece: part_copy(chunk, 0, piece).wait_send())
+
+
+def deliver_kernel(updated, src_out, rcv_out, cmp_out, sems):
+    rcv_terms, cmp_terms = rcv_out.shape[0], cmp_out.shape[0]
+    spans = (
+        (rcv_terms + cmp_terms, src_out.shape[0], src_out),
+        (0, rcv_terms, rcv_out),
+        (rcv_terms, cmp_terms, cmp_out),
+    )
+    copies = [
+        pltpu.make_async_copy(updated.at[pl.ds(start, size)], target, sems.at[i])
+        for i, (start, size, target) in enumerate(spans)
+    ]
+    for copy in copies:
+        copy.start()
+    for copy in copies:
+        copy.wait()
 
 
 def body(
@@ -517,12 +554,12 @@
     )
     held = [vmem(x.shape, x.dtype) for x in operands[:8]]
     held += [vmem((x.shape[0] * 128 // w, w), x.dtype) for x, w in zip(tables, (256, 128, 256, 128))]
-    return pl.pallas_call(
+    updated = pl.pallas_call(
         functools.partial(fused_kernel, (lines, plane, slot_cap, terms)),
-        out_shape=tuple(shape(x.shape, F32) for x in (src_filters, rcv_filters, cmp_filters)),
+        out_shape=shape((rows_all + 8, taps), F32),
         in_specs=[pl.BlockSpec(memory_space=pltpu.SMEM)]
         + [pl.BlockSpec(memory_space=pltpu.HBM)] * len(operands),
-        out_specs=(pl.BlockSpec(memory_space=pltpu.VMEM),) * 3,
+        out_specs=pl.BlockSpec(memory_space=pltpu.VMEM),
         scratch_shapes=held
         + [
             vmem((Z, rows_all, 128), F32),
@@ -546,10 +583,10 @@
             vmem((ROWS * blocks, 2 * taps), F32),
             sem((16,)),
             sem((plane,)), sem((plane,)),
-            sem((2, Z)), sem((2, Z + 1)),
+            sem((2, Z, 2)), sem((2, Z + 1, 2)),
             sem((Z, plane)), sem((Z, plane)),
             sem((Z, plane)), sem((Z, plane)),
-            sem((Z,)), sem((2, Z)),
+            sem((Z, 2)), sem((2, Z, 2)),
         ],
         compiler_params=pltpu.CompilerParams(
             vmem_limit_bytes=VMEM_LIMIT, collective_id=0, has_side_effects=True
@@ -558,6 +595,15 @@
             flops=16 * trace_rows * samples * taps, bytes_accessed=6 * 2**20, transcendentals=0
         ),
     )(counts, *operands)
+    anywhere = pl.BlockSpec(memory_space=pl.ANY)
+    return pl.pallas_call(
+        deliver_kernel,
+        out_shape=tuple(shape(x.shape, F32) for x in (src_filters, rcv_filters, cmp_filters)),
+        in_specs=[anywhere],
+        out_specs=(anywhere,) * 3,
+        scratch_shapes=[sem((3,))],
+        compiler_params=pltpu.CompilerParams(vmem_limit_bytes=VMEM_LIMIT),
+    )(updated)
 
 
 def solution(mesh):

time: 63.3 us -> 62.5 us (0.987); the launches traced: 63.1 us -> 61.5 us
  local copies, waits for them, and re-layouts: 4.27 us -> 0 us
  Pallas kernels: 57.5 us -> 60.1 us
    pallas_call x0 -> x1, Pallas kernels: none -> 7.15 us  [body(): pl.pallas_call(deliver_kernel, out_shape=tuple((shape(x.shape, F32) for x...]
    pallas_call x1, Pallas kernels: 57.5 us -> 52.9 us  [body(): pl.pallas_call(functools.partial(fused_kernel, (lines, plane, slot_cap, t...]
    unnamed x3 -> x0, local copies, waits for them, and re-layouts: 4.27 us -> none
where the time goes in v4:
time: 62.5 us; the launch traced here: 61.5 us
  Pallas kernels  60.1 us (96%)
  between operations  1.45 us (2%)
    pallas_call x1, Pallas kernels, body(): pl.pallas_call(functools.partial(fused_kernel, (lines, plane, slot_cap, t...  52.9 us
    pallas_call x1, Pallas kernels, body(): pl.pallas_call(deliver_kernel, out_shape=tuple((shape(x.shape, F32) for x...  7.15 us

profile of v4, /device:TPU:0, one launch (start us, length us, event | category | flops | bytes accessed | tf_op | source)
XLA Modules:
  0.0 61.5 jit_solution(14938140053845545224)
XLA Ops:
  1.3 52.9 %shard_map.166.updated = f32[392,128]{1,0:T(8,128)} custom-call(s32[1]{0:T(128)S(6)} %copy.18.counts, bf16[512,2048]{1,0:T(8,128)(2,1)} %traces.1, bf16[512,2048]{1,0:T(8,128)(2,1)} %targets.1, s32[1,512]{1,0:T(1,128)} %bitcast.7, s32[1,512]{1,0:T(1,128)} %bitcast.8, s32[1,512]{1,0:T(1,128)} %bitcast.9, s32[32,128]{1,0:T(8,128)} %bitcast.6, ...), custom_call_target="tpu_custom_call" | custom-call | flops 2147483648 | bytes 6291456 | tf_op jit(solution)/shard_map/pallas_call | solution.py:557
  54.2 7.1 %shard_map.167 = (f32[4,128]{1,0:T(4,128)}, f32[128,128]{1,0:T(8,128)}, f32[256,128]{1,0:T(8,128)}) custom-call(f32[392,128]{1,0:T(8,128)} %shard_map.166.updated), custom_call_target="tpu_custom_call" | custom-call | tf_op jit(solution)/shard_map/pallas_call | solution.py:599

commit v5 on v4

--- a/solution.py
+++ b/solution.py
@@ -13,6 +13,7 @@
 F32 = jnp.float32
 AXES = ("shot", "line")
 ROWS = 64
+PIECES = 3
 Z = 4
 VMEM_LIMIT = 60 * 1024 * 1024
 
@@ -252,19 +253,19 @@
         copy.start()
     pl.semaphore_wait(barrier, plane - 1 + Z - 1)
 
-    half = rows_all // 2
+    share = rows_all // PIECES
 
     def table_copy(way, distance, piece):
         chunk = z - distance if way == 0 else z + distance
         target = me + plane if way == 0 else me - plane
-        rows = table.at[chunk, pl.ds(piece * half, half)]
+        rows = table.at[chunk, pl.ds(piece * share, share)]
         return remote(
             rows, rows, tab_ss.at[way, distance, piece], tab_rs.at[way, distance + 1, piece], target
         )
 
     def table_wait(way, distance, piece):
         chunk = z - distance if way == 0 else z + distance
-        rows = table.at[chunk, pl.ds(piece * half, half)]
+        rows = table.at[chunk, pl.ds(piece * share, share)]
         remote(
             rows, rows, tab_ss.at[way, distance, piece], tab_rs.at[way, distance, piece], me
         ).wait_recv()
@@ -277,7 +278,7 @@
 
     copies[4].wait()
     copies[5].wait()
-    for piece in range(2):
+    for piece in range(PIECES):
         for way in range(2):
             pl.when(goes_on(way, 0))(lambda way=way, piece=piece: table_copy(way, 0, piece).start())
     for i in range(4):
@@ -386,7 +387,7 @@
 
     marks = [turns // 4, 5 * turns // 8, turns, turns]
     for distance in range(1, Z):
-        for piece in range(2):
+        for piece in range(PIECES):
             for way in range(2):
                 pl.when(arrives(way, distance))(lambda way=way, piece=piece: table_wait(way, distance, piece))
                 if distance < Z - 1:
@@ -435,8 +436,7 @@
         grad_recv[chunk, pl.ds(p, 1)] = grad_send[chunk, pl.ds(p, 1)]
     out[pl.ds(rows_all, 8)] = settled_src(v_src_f[...], src_hot, grads, src_energy)
 
-    cut = rows_all // 16 * 8
-    spans = (pl.ds(0, cut), pl.ds(cut, rows_all + 8 - cut))
+    spans = [pl.ds(i * share, share + (8 if i == PIECES - 1 else 0)) for i in range(PIECES)]
 
     def part_copy(chunk, way, piece):
         target = me + plane if way == 0 else me - plane
@@ -453,6 +453,12 @@
             part_rs.at[way, chunk, piece], me,
         ).wait_recv()
         part[chunk, rows] = part[chunk, rows] + inbox[way, chunk, rows]
+
+    def relay(chunk, way, add):
+        for piece in range(PIECES):
+            if add:
+                add_inbox(chunk, way, piece)
+            part_copy(chunk, way, piece).start()
 
     for step, chunk in enumerate(order):
         for offset in range(1, plane):
@@ -481,14 +487,16 @@
         for i in range(rows_all // 128):
             packed = packed + jnp.where(lines8 == i, energy[:, i * 128 : (i + 1) * 128], 0.0)
         part[chunk, pl.ds(rows_all, 8)] = packed
-        for piece in range(2):
-            def pass_on(way, chunk=chunk, piece=piece):
-                pl.when(z > 0 if way == 0 else z < Z - 1)(lambda: add_inbox(chunk, way, piece))
-                if step < Z - 1:
-                    part_copy(chunk, way, piece).start()
-
-            pl.when(chunk >= z)(lambda: pass_on(0))
-            pl.when(chunk <= z)(lambda: pass_on(1))
+        if step < Z - 1:
+            pl.when((chunk > z) & (z == 0))(lambda chunk=chunk: relay(chunk, 0, False))
+            pl.when((chunk < z) & (z == Z - 1))(lambda chunk=chunk: relay(chunk, 1, False))
+        if step:
+            before = order[step - 1]
+            pl.when((before > z) & (z > 0))(lambda before=before: relay(before, 0, True))
+            pl.when((before < z) & (z < Z - 1))(lambda before=before: relay(before, 1, True))
+    for piece in range(PIECES):
+        pl.when(z > 0)(lambda piece=piece: add_inbox(z, 0, piece))
+        pl.when(z < Z - 1)(lambda piece=piece: add_inbox(z, 1, piece))
 
     packed = part[z, pl.ds(rows_all, 8)]
     for i in range(rows_all // 128):
@@ -501,7 +509,7 @@
         copy.wait_send()
     for distance in range(Z - 1):
         for way in range(2):
-            for piece in range(2):
+            for piece in range(PIECES):
                 pl.when(goes_on(way, distance))(
                     lambda way=way, piece=piece: table_copy(way, distance, piece).wait_send()
                 )
@@ -509,25 +517,31 @@
         for offset in range(1, plane):
             value_copy(chunk, offset).wait_send()
             grad_copy(chunk, offset).wait_send()
-        for piece in range(2):
+        for piece in range(PIECES):
             pl.when(z != chunk)(lambda chunk=chunk, piece=piece: part_copy(chunk, 0, piece).wait_send())
 
 
-def deliver_kernel(updated, src_out, rcv_out, cmp_out, sems):
+def deliver_kernel(updated, src_out, rcv_out, cmp_out, held, sems):
     rcv_terms, cmp_terms = rcv_out.shape[0], cmp_out.shape[0]
     spans = (
         (rcv_terms + cmp_terms, src_out.shape[0], src_out),
         (0, rcv_terms, rcv_out),
         (rcv_terms, cmp_terms, cmp_out),
     )
-    copies = [
-        pltpu.make_async_copy(updated.at[pl.ds(start, size)], target, sems.at[i])
-        for i, (start, size, target) in enumerate(spans)
-    ]
-    for copy in copies:
-        copy.start()
-    for copy in copies:
-        copy.wait()
+    loads, stores = [], []
+    for i, (start, size, target) in enumerate(spans):
+        padded = (size + 7) // 8 * 8
+        loads.append(
+            pltpu.make_async_copy(updated.at[pl.ds(start, padded)], held.at[pl.ds(start, padded)], sems.at[0, i])
+        )
+        stores.append(pltpu.make_async_copy(held.at[pl.ds(start, size)], target, sems.at[1, i]))
+    for load in loads:
+        load.start()
+    for load, store in zip(loads, stores):
+        load.wait()
+        store.start()
+    for store in stores:
+        store.wait()
 
 
 def body(
@@ -583,10 +597,10 @@
             vmem((ROWS * blocks, 2 * taps), F32),
             sem((16,)),
             sem((plane,)), sem((plane,)),
-            sem((2, Z, 2)), sem((2, Z + 1, 2)),
+            sem((2, Z, PIECES)), sem((2, Z + 1, PIECES)),
             sem((Z, plane)), sem((Z, plane)),
             sem((Z, plane)), sem((Z, plane)),
-            sem((Z, 2)), sem((2, Z, 2)),
+            sem((Z, PIECES)), sem((2, Z, PIECES)),
         ],
         compiler_params=pltpu.CompilerParams(
             vmem_limit_bytes=VMEM_LIMIT, collective_id=0, has_side_effects=True
@@ -601,7 +615,7 @@
         out_shape=tuple(shape(x.shape, F32) for x in (src_filters, rcv_filters, cmp_filters)),
         in_specs=[anywhere],
         out_specs=(anywhere,) * 3,
-        scratch_shapes=[sem((3,))],
+        scratch_shapes=[vmem((rows_all + 8, taps), F32), sem((2, 3))],
         compiler_params=pltpu.CompilerParams(vmem_limit_bytes=VMEM_LIMIT),
     )(updated)
 

time: 62.5 us -> 56.6 us (0.906)
  the two profiles are of different devices: /device:TPU:0 before, /device:TPU:9 now
where the time goes in v5:
time: 56.6 us; the launch traced here: 56.4 us
  Pallas kernels  54.9 us (97%)
  between operations  1.45 us (3%)
    pallas_call x1, Pallas kernels, body(): pl.pallas_call(functools.partial(fused_kernel, (lines, plane, slot_cap, t...  53.3 us
    pallas_call x1, Pallas kernels, body(): pl.pallas_call(deliver_kernel, out_shape=tuple((shape(x.shape, F32) for x...  1.66 us

profile of v5, /device:TPU:9, one launch (start us, length us, event | category | flops | bytes accessed | tf_op | source)
XLA Modules:
  0.0 56.4 jit_solution(7432440745165970310)
XLA Ops:
  1.3 53.3 %shard_map.166.updated = f32[392,128]{1,0:T(8,128)} custom-call(s32[1]{0:T(128)S(6)} %copy.18.counts, bf16[512,2048]{1,0:T(8,128)(2,1)} %traces.1, bf16[512,2048]{1,0:T(8,128)(2,1)} %targets.1, s32[1,512]{1,0:T(1,128)} %bitcast.7, s32[1,512]{1,0:T(1,128)} %bitcast.8, s32[1,512]{1,0:T(1,128)} %bitcast.9, s32[32,128]{1,0:T(8,128)} %bitcast.6, ...), custom_call_target="tpu_custom_call" | custom-call | flops 2147483648 | bytes 6291456 | tf_op jit(solution)/shard_map/pallas_call | solution.py:571
  54.6 1.7 %shard_map.167 = (f32[4,128]{1,0:T(4,128)}, f32[128,128]{1,0:T(8,128)}, f32[256,128]{1,0:T(8,128)}) custom-call(f32[392,128]{1,0:T(8,128)} %shard_map.166.updated), custom_call_target="tpu_custom_call" | custom-call | tf_op jit(solution)/shard_map/pallas_call | solution.py:613
